TPU v7x, 128 devices: a whole 4x4x4 slice. The times are simulated.
128 devices in a mesh: gx: 8 (over y, core), gy: 16 (over z, x).
Axes of the slice: x: 4, y: 4, z: 4, core: 2. Of those that a mesh axis runs over, the one named last changes fastest.
Arguments:
- q_now: float32 [5, 128, 256, 256], P(None, 'gx', 'gy'), may hold values from -6 to 6
- q_prev: float32 [5, 128, 256, 256], P(None, 'gx', 'gy'), may hold values from -6 to 6
- jacobian: float32 [128, 256, 256], P('gx', 'gy'), may hold values from 0.5 to 2
- flux_split: float32 [3, 2, 5, 5], replicated, may hold values from -2 to 2
- donor_base: int32 [131072], P(('gx', 'gy')), may hold values from 0 to 57374
- donor_frac: float32 [3, 131072], P(None, ('gx', 'gy')), may hold values from 0 to 1
- fringe_dest: int32 [131072, 1], P(('gx', 'gy')), may hold values from 0 to 127; in each aligned block of 1024 rows (0 to 1023, 1024 to 2047, ...) at most 16 rows name the same one
- receptor_cell: int32 [131072], P(('gx', 'gy')), may hold values from 0 to 65535
- fringe_count: int32 [128], P(('gx', 'gy')), may hold values from 1 to 1024, 98304 in all
Outputs:
- q_next: float32 [5, 128, 256, 256], P(None, 'gx', 'gy')
Inputs may be any that keep to these rules, and one draw needn't show every extreme that they name: `fringe_dest`: among the 1024 rows of one block, at most 16 name the same destination block; some block sends exactly 16 to one destination. A block's live rows are its first fringe_count rows; the counts sum to 98304 and some block has 1024. `receptor_cell`: several rows may share a receptor cell.
All inputs are finite; a program needn't handle non-finite values.
Results may differ from a plain program's by a relative error of at most 0.0003.
Values sent between devices are 32-bit elements; how exact they have to be, the bound alone decides.
A program may use at most 192 MiB of HBM per device.

v0:
```python
import jax
import jax.numpy as jnp
from jax import lax
from jax.experimental import pallas as pl
from jax.experimental.pallas import tpu as pltpu
from jax.sharding import PartitionSpec as P

MESH = pl.DeviceIdType.MESH
F32 = jnp.float32
BF16 = jnp.bfloat16
V, CX, CY, CZ = 5, 16, 16, 256
ROWS = 1024
NDEV = 128
CAP = 16
GX, GY = 8, 16
VY = V * CY
CHUNK = 256
LIMIT = 48 * 1024 * 1024


def iota(shape, dim):
    return lax.broadcasted_iota(jnp.int32, shape, dim)


def two(a):
    hi = a.astype(BF16)
    return hi, (a - hi.astype(F32)).astype(BF16)


def dot(a, b):
    return lax.dot_general(a, b, (((1,), (0,)), ((), ())), preferred_element_type=F32)


def dot_t(a, b):
    return lax.dot_general(a, b, (((1,), (1,)), ((), ())), preferred_element_type=F32)


def flux_matrix(flux):
    col = iota((1, 256), 1)
    block = (col >= 80).astype(jnp.int32) + (col >= 160).astype(jnp.int32) + (col >= 240).astype(jnp.int32)
    side = (col >= 248).astype(jnp.int32)
    var = jnp.where(block == 3, col - 240 - 8 * side, (col >> 4) - 5 * block)
    yc = jnp.where(block == 3, 17 * side - 1, col & 15)
    y = iota((CY, 256), 0)
    here = (yc == y).astype(F32)
    back = (yc == y - 1).astype(F32)
    fwd = (yc == y + 1).astype(F32)
    mid = (block == 1).astype(F32)
    near = ((block == 1) | (block == 3)).astype(F32)
    w_mid, w_back, w_fwd = here * mid, back * near, fwd * near
    w_left, w_right = here * (block == 0).astype(F32), here * (block == 2).astype(F32)
    mains, ups, downs = [], [], []
    for a in range(V):
        row = {}
        for d in range(3):
            for s in range(2):
                total = jnp.zeros((1, 256), F32)
                for b in range(V):
                    total = jnp.where(var == b, flux[((d * 2 + s) * V + a) * V + b], total)
                row[d, s] = total
        centre = (row[0, 0] - row[0, 1]) + (row[1, 0] - row[1, 1]) + (row[2, 0] - row[2, 1])
        mains.append(
            centre * w_mid - row[1, 0] * w_back + row[1, 1] * w_fwd - row[0, 0] * w_left + row[0, 1] * w_right
        )
        ups.append(row[2, 1] * w_mid)
        downs.append(row[2, 0] * w_mid)
    return jnp.concatenate(mains + ups + downs, axis=0)


def y_faces(planes):
    n = planes[0].shape[0]
    pad = [jnp.zeros((n, 8 - V, CZ), F32)]
    return [jnp.concatenate([p[:, y : y + 1, :] for p in planes] + pad, axis=1) for y in (0, CY - 1)]


def donate(count, flux, q_now, q_prev, base, frac, dest, cell, out, face_x, face_y, km_hi, km_lo, qq):
    planes = [q_now[v] for v in range(V)]
    lo_y, hi_y = y_faces(planes)
    face_y[0] = lo_y
    face_y[1] = hi_y
    for v in range(V):
        face_x[0, v * CY : (v + 1) * CY, :] = q_now[v, 0]
        face_x[1, v * CY : (v + 1) * CY, :] = q_now[v, CX - 1]
    hi, lo = two(flux_matrix(flux))
    km_hi[...] = hi
    km_lo[...] = lo
    for f, ref in enumerate((q_prev, q_now)):
        for v in range(V):
            hi, lo = two(ref[v].reshape(CX * CY, CZ))
            qq[f * V + v, :, 0:CZ] = hi
            qq[f * V + v, :, CZ:] = lo

    live = iota((1, ROWS), 1) < count[0]
    where_to = jnp.where(live, dest[...], NDEV)
    onehot = (iota((NDEV, ROWS), 0) == where_to).astype(F32)
    onehot_b = onehot.astype(BF16)
    before = (iota((CHUNK, CHUNK), 0) < iota((CHUNK, CHUNK), 1)).astype(F32).astype(BF16)
    ones = jnp.ones((CHUNK, CHUNK), BF16)
    carry = jnp.zeros((NDEV, CHUNK), F32)
    slots = []
    for c in range(ROWS // CHUNK):
        part = onehot_b[:, c * CHUNK : (c + 1) * CHUNK]
        rank = dot(part, before) + carry
        carry = carry + dot(part, ones)
        slots.append(jnp.sum(rank * onehot[:, c * CHUNK : (c + 1) * CHUNK], axis=0, keepdims=True))

    packed = jnp.zeros((22 * CAP, NDEV), F32)
    for c in range(ROWS // CHUNK):
        span = slice(c * CHUNK, (c + 1) * CHUNK)
        low = base[:, span]
        base_x = low // ((CZ - 1) * (CY - 1))
        rest = low - base_x * ((CZ - 1) * (CY - 1))
        base_y = rest // (CZ - 1)
        base_z = rest - base_y * (CZ - 1)
        fx, fy, fz = frac[0:1, span], frac[1:2, span], frac[2:3, span]

        def hat(n, low, f, rest):
            at = iota((n, CHUNK), 0)
            return jnp.where(at == low, rest, jnp.where(at == low + 1, f, jnp.zeros_like(f)))

        z_hi, z_lo = two(hat(CZ, base_z, fz, 1.0 - fz))
        w_x, w_y = hat(CX, base_x, fx, 1.0 - fx), hat(CY, base_y, fy, 1.0 - fy)
        w_xy = jnp.concatenate([w_x[x : x + 1] * w_y for x in range(CX)], axis=0)
        values = []
        for f in range(2):
            left = qq[f * V : (f + 1) * V].reshape(V * CX * CY, 2 * CZ)
            along = dot(left, jnp.concatenate([z_hi, z_hi], axis=0)) + dot(left[:, 0:CZ], z_lo)
            for v in range(V):
                values.append(jnp.sum(along[v * 256 : (v + 1) * 256] * w_xy, axis=0, keepdims=True))
        cells = cell[:, span]
        rows_hi, rows_lo = [], []
        at_slot = (iota((CAP, CHUNK), 0).astype(F32) == slots[c]).astype(F32)
        for value in values:
            hi = value.astype(BF16).astype(F32)
            rows_hi.append((at_slot * hi).astype(BF16))
            rows_lo.append((at_slot * (value - hi)).astype(BF16))
        xy = ((cells >> 8) + 1).astype(F32)
        z = (cells & 255).astype(F32)
        left = jnp.concatenate(
            rows_hi + [(at_slot * xy).astype(BF16), (at_slot * z).astype(BF16)] + rows_lo, axis=0
        )
        packed = packed + dot_t(left, onehot_b[:, span])
    half = 2 * V * CAP
    full = jnp.concatenate(
        [packed[:half] + packed[half + 2 * CAP :], packed[half : half + 2 * CAP], jnp.zeros((4 * CAP, NDEV), F32)], axis=0
    )
    for h in range(2):
        out[:, :, h, :] = full[h * 128 : (h + 1) * 128].T.reshape(GX, GY, 128)


def split_planes(qs_hi, qs_lo, halo_x, halo_y, hs_hi, hs_lo):
    ix, iy = lax.axis_index("gx"), lax.axis_index("gy")
    nx, ny = lax.axis_size("gx"), lax.axis_size("gy")
    for side, plane, there in ((0, 0, ix > 0), (1, CX + 1, ix < nx - 1)):
        keep = jnp.where(there, 1.0, 0.0)
        hi, lo = two(halo_x[side] * keep)
        qs_hi[plane] = hi
        qs_lo[plane] = lo
    keep = [jnp.where(iy > 0, 1.0, 0.0), jnp.where(iy < ny - 1, 1.0, 0.0)]
    hi, lo = two(jnp.concatenate([halo_y[side] * keep[side] for side in range(2)], axis=1))
    hs_hi[...] = hi
    hs_lo[...] = lo


def flux_of(x, km_hi, km_lo, qs_hi, qs_lo, hs_hi, hs_lo):
    right_hi = jnp.concatenate([qs_hi[x], qs_hi[x + 1], qs_hi[x + 2], hs_hi[x]], axis=0)
    right_lo = jnp.concatenate([qs_lo[x], qs_lo[x + 1], qs_lo[x + 2], hs_lo[x]], axis=0)
    total = dot(km_hi[...], right_hi) + dot(km_lo[...], right_hi) + dot(km_hi[...], right_lo)
    z = iota((VY, CZ), 1)
    fwd = jnp.where(z == CZ - 1, 0.0, pltpu.roll(total[VY : 2 * VY], CZ - 1, 1))
    back = jnp.where(z == 0, 0.0, pltpu.roll(total[2 * VY :], 1, 1))
    return total[:VY] + fwd - back


def first(got, q_now, q_prev, jac, halo_x, halo_y, km_hi, km_lo, state, later, face_x, face_y,
          qs_hi, qs_lo, hs_hi, hs_lo, parts, places, at_z):
    for x in range(CX):
        for v in range(V):
            hi, lo = two(q_now[v, x])
            qs_hi[x + 1, v * CY : (v + 1) * CY, :] = hi
            qs_lo[x + 1, v * CY : (v + 1) * CY, :] = lo
    split_planes(qs_hi, qs_lo, halo_x, halo_y, hs_hi, hs_lo)

    halves = [got[:, :, h, :].reshape(NDEV, 128) for h in range(2)]
    turned = jnp.concatenate([h.T for h in halves], axis=0)
    for s in range(CAP):
        lanes = slice(s * NDEV, (s + 1) * NDEV)
        for g in range(2):
            for v in range(V):
                row = turned[(g * V + v) * CAP + s :][:1]
                hi, lo = two(jnp.broadcast_to(row, (CY, NDEV)))
                parts[g * 11 + v, :, lanes] = hi
                parts[g * 11 + V + v, :, lanes] = lo
        parts[10, :, lanes] = jnp.ones((CY, NDEV), BF16)
        places[:, lanes] = jnp.broadcast_to(turned[10 * CAP + s :][:1], (CY, NDEV))
        column = halves[1][:, 3 * CAP + s : 3 * CAP + s + 1]
        at_z[lanes, :] = (iota((NDEV, CZ), 1).astype(F32) == column).astype(F32).astype(BF16)

    def plane(x, carry):
        mark = (iota((CY, 1), 0) + (x * CY + 1)).astype(F32)
        here = (places[...] == mark).astype(F32).astype(BF16)
        left = jnp.concatenate([parts[i] * here for i in range(21)], axis=0)
        landed = dot(left, at_z[...])
        flux = flux_of(x, km_hi, km_lo, qs_hi, qs_lo, hs_hi, hs_lo)
        scale = 0.2 * jac[x]
        hits = landed[10 * CY : 11 * CY]
        fresh = []
        for v in range(V):
            rows = slice(v * CY, (v + 1) * CY)
            q, qp = q_now[v, x], q_prev[v, x]
            g1 = landed[v * CY : (v + 1) * CY] + landed[(V + v) * CY : (V + v + 1) * CY]
            g2 = landed[(11 + v) * CY : (12 + v) * CY] + landed[(16 + v) * CY : (17 + v) * CY]
            w = q - scale * (flux[rows] + (qp - q) + 2.0 * (hits * q - g1))
            state[x, rows, :] = w
            later[x, rows, :] = w - scale * ((3.0 * w - 4.0 * q + qp) + 2.0 * (hits * w - g2))
            fresh.append(w[None])
        lo_y, hi_y = y_faces(fresh)
        face_y[0, x] = lo_y[0]
        face_y[1, x] = hi_y[0]
        return carry

    lax.fori_loop(0, CX, plane, 0)
    face_x[0] = state[0]
    face_x[1] = state[CX - 1]


def second(state, later, jac, halo_x, halo_y, km_hi, km_lo, out, qs_hi, qs_lo, hs_hi, hs_lo):
    for x in range(CX):
        hi, lo = two(state[x])
        qs_hi[x + 1] = hi
        qs_lo[x + 1] = lo
    split_planes(qs_hi, qs_lo, halo_x, halo_y, hs_hi, hs_lo)

    def plane(x, carry):
        flux = flux_of(x, km_hi, km_lo, qs_hi, qs_lo, hs_hi, hs_lo)
        scale = 0.2 * jac[x]
        for v in range(V):
            rows = slice(v * CY, (v + 1) * CY)
            out[v, x] = later[x, rows, :] - scale * flux[rows]
        return carry

    lax.fori_loop(0, CX, plane, 0)


def face_copies(ix, iy, face_x, face_y, halo_x, halo_y, send, recv):
    copies = []
    for side in range(2):
        step = 2 * side - 1
        peer_x = lax.rem(ix + step + GX, GX)
        peer_y = lax.rem(iy + step + GY, GY)
        copies.append(
            pltpu.make_async_remote_copy(
                face_x.at[side], halo_x.at[1 - side], send.at[side], recv.at[side],
                device_id=(peer_x, iy), device_id_type=MESH,
            )
        )
        copies.append(
            pltpu.make_async_remote_copy(
                face_y.at[side], halo_y.at[1 - side], send.at[2 + side], recv.at[2 + side],
                device_id=(ix, peer_y), device_id_type=MESH,
            )
        )
    return copies


def exchange(sent, face_x, face_y, got, halo_x, halo_y, mid, send, recv, send_a, recv_a, send_b, recv_b):
    ix, iy = lax.axis_index("gx"), lax.axis_index("gy")
    peers = [(lax.rem(ix + k, GX), iy) for k in range(1, GX)] + [(ix, lax.rem(iy + k, GY)) for k in range(1, GY)]
    barrier = pltpu.get_barrier_semaphore()
    for peer in peers:
        pl.semaphore_signal(barrier, inc=1, device_id=peer, device_id_type=MESH)
    pl.semaphore_wait(barrier, len(peers))
    along = []
    for k in range(1, GX):
        to = lax.rem(ix + k, GX)
        copy = pltpu.make_async_remote_copy(
            sent.at[to], mid.at[ix], send_a.at[k - 1], recv_a.at[k - 1], device_id=(to, iy), device_id_type=MESH
        )
        copy.start()
        along.append(copy)
    faces = face_copies(ix, iy, face_x, face_y, halo_x, halo_y, send, recv)
    for copy in faces:
        copy.start()
    mid[ix] = sent[ix]
    for copy in along:
        copy.wait_recv()
    across = []
    for k in range(1, GY):
        to = lax.rem(iy + k, GY)
        copy = pltpu.make_async_remote_copy(
            mid.at[:, to], got.at[iy], send_b.at[k - 1], recv_b.at[k - 1], device_id=(ix, to), device_id_type=MESH
        )
        copy.start()
        across.append(copy)
    got[iy] = mid[:, iy]
    for copy in along:
        copy.wait_send()
    for copy in faces + across:
        copy.wait()


def neighbours(face_x, face_y, halo_x, halo_y, send, recv):
    ix, iy = lax.axis_index("gx"), lax.axis_index("gy")
    barrier = pltpu.get_barrier_semaphore()
    for step in (-1, 1):
        for peer in ((lax.rem(ix + step + GX, GX), iy), (ix, lax.rem(iy + step + GY, GY))):
            pl.semaphore_signal(barrier, inc=1, device_id=peer, device_id_type=MESH)
    pl.semaphore_wait(barrier, 4)
    faces = face_copies(ix, iy, face_x, face_y, halo_x, halo_y, send, recv)
    for copy in faces:
        copy.start()
    for copy in faces:
        copy.wait()


VM = pl.BlockSpec(memory_space=pltpu.VMEM)
SM = pl.BlockSpec(memory_space=pltpu.SMEM)
FACES = [jax.ShapeDtypeStruct((2, VY, CZ), F32), jax.ShapeDtypeStruct((2, CX, 8, CZ), F32)]
MATRIX = [jax.ShapeDtypeStruct((3 * VY, 256), BF16)] * 2
PLANES = [pltpu.VMEM((CX + 2, VY, CZ), BF16)] * 2 + [pltpu.VMEM((CX, 16, CZ), BF16)] * 2


def call_donate(count, flux, q_now, q_prev, base, frac, dest, cell):
    return pl.pallas_call(
        donate,
        out_shape=[jax.ShapeDtypeStruct((GX, GY, 2, 128), F32)] + FACES + MATRIX,
        in_specs=[SM, SM] + [VM] * 6,
        out_specs=[VM] * 5,
        scratch_shapes=[pltpu.VMEM((2 * V, CX * CY, 2 * CZ), BF16)],
        compiler_params=pltpu.CompilerParams(vmem_limit_bytes=LIMIT),
        name="donate",
    )(count, flux, q_now, q_prev, base, frac, dest, cell)


def call_exchange(sent, face_x, face_y):
    return pl.pallas_call(
        exchange,
        out_shape=[jax.ShapeDtypeStruct((GY, GX, 2, 128), F32)] + FACES,
        in_specs=[VM] * 3,
        out_specs=[VM] * 3,
        scratch_shapes=[pltpu.VMEM((GX, GY, 2, 128), F32)]
        + [pltpu.SemaphoreType.DMA((4,))] * 2
        + [pltpu.SemaphoreType.DMA((GX - 1,))] * 2
        + [pltpu.SemaphoreType.DMA((GY - 1,))] * 2,
        compiler_params=pltpu.CompilerParams(vmem_limit_bytes=LIMIT, collective_id=0, has_side_effects=True),
        name="exchange",
    )(sent, face_x, face_y)


def call_first(got, q_now, q_prev, jac, halo_x, halo_y, km_hi, km_lo):
    return pl.pallas_call(
        first,
        out_shape=[jax.ShapeDtypeStruct((CX, VY, CZ), F32)] * 2 + FACES,
        in_specs=[VM] * 8,
        out_specs=[VM] * 4,
        scratch_shapes=PLANES
        + [
            pltpu.VMEM((21, CY, NDEV * CAP), BF16),
            pltpu.VMEM((CY, NDEV * CAP), F32),
            pltpu.VMEM((NDEV * CAP, CZ), BF16),
        ],
        compiler_params=pltpu.CompilerParams(vmem_limit_bytes=LIMIT),
        name="first",
    )(got, q_now, q_prev, jac, halo_x, halo_y, km_hi, km_lo)


def call_neighbours(face_x, face_y):
    return pl.pallas_call(
        neighbours,
        out_shape=FACES,
        in_specs=[VM] * 2,
        out_specs=[VM] * 2,
        scratch_shapes=[pltpu.SemaphoreType.DMA((4,))] * 2,
        compiler_params=pltpu.CompilerParams(vmem_limit_bytes=LIMIT, collective_id=1, has_side_effects=True),
        name="neighbours",
    )(face_x, face_y)


def call_second(state, later, jac, halo_x, halo_y, km_hi, km_lo):
    return pl.pallas_call(
        second,
        out_shape=jax.ShapeDtypeStruct((V, CX, CY, CZ), F32),
        in_specs=[VM] * 7,
        out_specs=VM,
        scratch_shapes=PLANES,
        compiler_params=pltpu.CompilerParams(vmem_limit_bytes=LIMIT),
        name="second",
    )(state, later, jac, halo_x, halo_y, km_hi, km_lo)


def body(q_now, q_prev, jacobian, flux_split, donor_base, donor_frac, fringe_dest, receptor_cell, fringe_count):
    sent, face_x, face_y, km_hi, km_lo = call_donate(
        fringe_count, flux_split.reshape(-1), q_now, q_prev, donor_base.reshape(1, ROWS), donor_frac,
        fringe_dest.reshape(1, ROWS), receptor_cell.reshape(1, ROWS),
    )
    got, halo_x, halo_y = call_exchange(sent, face_x, face_y)
    state, later, face_x, face_y = call_first(got, q_now, q_prev, jacobian, halo_x, halo_y, km_hi, km_lo)
    halo_x, halo_y = call_neighbours(face_x, face_y)
    return call_second(state, later, jacobian, halo_x, halo_y, km_hi, km_lo)


def solution(mesh):
    return jax.shard_map(
        body,
        mesh=mesh,
        in_specs=(
            P(None, "gx", "gy", None),
            P(None, "gx", "gy", None),
            P("gx", "gy", None),
            P(),
            P(("gx", "gy")),
            P(None, ("gx", "gy")),
            P(("gx", "gy"), None),
            P(("gx", "gy")),
            P(("gx", "gy")),
        ),
        out_specs=P(None, "gx", "gy", None),
        check_vma=False,
    )
```

profile of v0, /device:TPU:0, one launch (start us, length us, event | category | flops | bytes accessed | tf_op | source)
XLA Modules:
  0.0 61.6 jit_solution(1108993674421019877)
XLA Ops:
  0.7 0.7 %copy.10 = f32[3,2,5,5]{3,2,1,0:T(8,128)S(1)} copy(f32[3,2,5,5]{3,1,2,0:T(2,128)} %param.12) | data formatting | bytes 1200 | tf_op args[3]
  1.4 0.1 reshape.12.flux
  1.5 0.0 copy-start
  1.5 1.3 %copy-done = f32[5,16,16,256]{3,2,1,0:T(8,128)S(1)} copy-done((f32[5,16,16,256]{3,2,1,0:T(8,128)S(1)}, f32[5,16,16,256]{3,2,1,0:T(8,128)}, u32[]{:S(2)}) %copy-start) | copy-done | bytes 1310744
  2.8 0.0 copy-start.2
  2.8 1.3 %copy-done.2 = f32[5,16,16,256]{3,2,1,0:T(8,128)S(1)} copy-done((f32[5,16,16,256]{3,2,1,0:T(8,128)S(1)}, f32[5,16,16,256]{3,2,1,0:T(8,128)}, u32[]{:S(2)}) %copy-start.2) | copy-done | bytes 1310744
  4.1 0.0 copy-start.4
  4.1 0.7 %copy-done.4 = f32[3,1024]{1,0:T(4,128)S(1)} copy-done((f32[3,1024]{1,0:T(4,128)S(1)}, f32[3,1024]{1,0:T(4,128)}, u32[]{:S(2)}) %copy-start.4) | copy-done | bytes 12312
  4.8 0.0 copy-start.5
  4.8 0.7 %copy-done.5 = s32[1024]{0:T(1024)S(1)} copy-done((s32[1024]{0:T(1024)S(1)}, s32[1024]{0:T(1024)}, u32[]{:S(2)}) %copy-start.5) | copy-done | bytes 4120
  5.5 0.0 copy-start.6
  5.5 0.7 %copy-done.6 = s32[1024,1]{0,1:T(1,128)S(1)} copy-done((s32[1024,1]{0,1:T(1,128)S(1)}, s32[1024,1]{0,1:T(1,128)}, u32[]{:S(2)}) %copy-start.6) | copy-done | bytes 4120
  6.2 0.0 copy-start.7
  6.2 0.7 %copy-done.7 = s32[1024]{0:T(1024)S(1)} copy-done((s32[1024]{0:T(1024)S(1)}, s32[1024]{0:T(1024)}, u32[]{:S(2)}) %copy-start.7) | copy-done | bytes 4120
  6.9 0.0 copy-start.1
  6.9 0.0 copy-start.3
  6.9 6.3 %donate.1 = (f32[8,16,2,128]{3,2,1,0:T(2,128)S(1)}, f32[2,80,256]{2,1,0:T(8,128)S(1)}, f32[2,16,8,256]{3,2,1,0:T(8,128)S(1)}, bf16[240,256]{1,0:T(8,128)(2,1)S(1)}, bf16[240,256]{1,0:T(8,128)(2,1)S(1)}) custom-call(s32[1]{0:T(128)S(6)} %copy.11.count, f32[150]{0:T(256)S(1)} %reshape.12.flux, f32[5,16,16,256]{3,2,1,0:T(8,128)S(1)} %copy-done, ...), custom_call_target="tpu_custom_call" | custom-call | tf_op jit(solution)/shard_map/donate/pallas_call | solution.py:324
  13.2 17.3 %exchange.1 = (f32[16,8,2,128]{3,2,1,0:T(2,128)S(1)}, f32[2,80,256]{2,1,0:T(8,128)S(1)}, f32[2,16,8,256]{3,2,1,0:T(8,128)S(1)}) custom-call(f32[8,16,2,128]{3,2,1,0:T(2,128)S(1)} %get-tuple-element.19.sent, f32[2,80,256]{2,1,0:T(8,128)S(1)} %get-tuple-element.20.face_x, f32[2,16,8,256]{3,2,1,0:T(8,128)S(1)} %get-tuple-element.21.face_y), custom_call_target="tpu_custom_call" | custom-call | tf_op jit(solution)/shard_map/exchange/pallas_call | solution.py:336
  30.5 0.0 copy-done.1
  30.5 0.0 copy-done.3
  30.5 15.9 %first.1 = (f32[16,80,256]{2,1,0:T(8,128)S(1)}, f32[16,80,256]{2,1,0:T(8,128)S(1)}, f32[2,80,256]{2,1,0:T(8,128)S(1)}, f32[2,16,8,256]{3,2,1,0:T(8,128)S(1)}) custom-call(f32[16,8,2,128]{3,2,1,0:T(2,128)S(1)} %get-tuple-element.22.got, f32[5,16,16,256]{3,2,1,0:T(8,128)S(1)} %copy-done.1, f32[5,16,16,256]{3,2,1,0:T(8,128)} %q_prev.3, ...), custom_call_target="tpu_custom_call" | custom-call | tf_op jit(solution)/shard_map/first/pallas_call | solution.py:351
  46.4 8.5 %neighbours.1 = (f32[2,80,256]{2,1,0:T(8,128)S(1)}, f32[2,16,8,256]{3,2,1,0:T(8,128)S(1)}) custom-call(f32[2,80,256]{2,1,0:T(8,128)S(1)} %get-tuple-element.29.face_x, f32[2,16,8,256]{3,2,1,0:T(8,128)S(1)} %get-tuple-element.30.face_y), custom_call_target="tpu_custom_call" | custom-call | tf_op jit(solution)/shard_map/neighbours/pallas_call | solution.py:368
  54.9 6.8 %second.1 = f32[5,16,16,256]{3,2,1,0:T(8,128)} custom-call(f32[16,80,256]{2,1,0:T(8,128)S(1)} %get-tuple-element.27.state, f32[16,80,256]{2,1,0:T(8,128)S(1)} %get-tuple-element.28.later, f32[16,16,256]{2,1,0:T(8,128)S(1)} %copy-done.3, f32[2,80,256]{2,1,0:T(8,128)S(1)} %get-tuple-element.31.halo_x, f32[2,16,8,256]{3,2,1,0:T(8,128)S(1)} %get-tuple-element.32.halo_y, ...), custom_call_target="tpu_custom_call" | custom-call | tf_op jit(solution)/shard_map/second/pallas_call | solution.py:380
Async XLA Ops:
  1.5 1.3 %copy-start = (f32[5,16,16,256]{3,2,1,0:T(8,128)S(1)}, f32[5,16,16,256]{3,2,1,0:T(8,128)}, u32[]{:S(2)}) copy-start(f32[5,16,16,256]{3,2,1,0:T(8,128)} %q_now.3) | copy-start | bytes 3932164
  2.8 1.3 %copy-start.2 = (f32[5,16,16,256]{3,2,1,0:T(8,128)S(1)}, f32[5,16,16,256]{3,2,1,0:T(8,128)}, u32[]{:S(2)}) copy-start(f32[5,16,16,256]{3,2,1,0:T(8,128)} %q_prev.3) | copy-start | bytes 3932164
  4.1 0.7 %copy-start.4 = (f32[3,1024]{1,0:T(4,128)S(1)}, f32[3,1024]{1,0:T(4,128)}, u32[]{:S(2)}) copy-start(f32[3,1024]{1,0:T(4,128)} %frac.1) | copy-start | bytes 36868
  4.8 0.7 %copy-start.5 = (s32[1024]{0:T(1024)S(1)}, s32[1024]{0:T(1024)}, u32[]{:S(2)}) copy-start(s32[1024]{0:T(1024)} %param.13) | copy-start | bytes 12292
  5.5 0.7 %copy-start.6 = (s32[1024,1]{0,1:T(1,128)S(1)}, s32[1024,1]{0,1:T(1,128)}, u32[]{:S(2)}) copy-start(s32[1024,1]{0,1:T(1,128)} %param.15) | copy-start | bytes 12292
  6.2 0.7 %copy-start.7 = (s32[1024]{0:T(1024)S(1)}, s32[1024]{0:T(1024)}, u32[]{:S(2)}) copy-start(s32[1024]{0:T(1024)} %param.16) | copy-start | bytes 12292
  6.9 23.6 %copy-start.1 = (f32[5,16,16,256]{3,2,1,0:T(8,128)S(1)}, f32[5,16,16,256]{3,2,1,0:T(8,128)}, u32[]{:S(2)}) copy-start(f32[5,16,16,256]{3,2,1,0:T(8,128)} %q_now.3) | copy-start | bytes 3932164
  6.9 23.6 %copy-start.3 = (f32[16,16,256]{2,1,0:T(8,128)S(1)}, f32[16,16,256]{2,1,0:T(8,128)}, u32[]{:S(2)}) copy-start(f32[16,16,256]{2,1,0:T(8,128)} %jac.3) | copy-start | bytes 786436
where the time goes:
time: 62 us; the launch traced here: 61.6 us
  Pallas kernels  54.7 us (88%)
  local copies, waits for them, and re-layouts  6.24 us (10%)
  between operations  0.72 us (1%)
    pallas_call x1, Pallas kernels, call_exchange(): pl.pallas_call(exchange, out_shape=[jax.ShapeDtypeStruct((GY, GX, 2, 128)...  17.3 us
    pallas_call x1, Pallas kernels, call_first(): pl.pallas_call(first, out_shape=[jax.ShapeDtypeStruct((CX, VY, CZ), F32)]...  15.9 us
    pallas_call x1, Pallas kernels, call_neighbours(): pl.pallas_call(neighbours, out_shape=FACES, in_specs=[VM] * 2, out_specs=...  8.45 us
    pallas_call x1, Pallas kernels, call_second(): pl.pallas_call(second, out_shape=jax.ShapeDtypeStruct((V, CX, CY, CZ), F3...  6.75 us
    pallas_call x1, Pallas kernels, call_donate(): pl.pallas_call(donate, out_shape=[jax.ShapeDtypeStruct((GX, GY, 2, 128),...  6.32 us
    unnamed x17, local copies, waits for them, and re-layouts  6.13 us

commit v1 on v0

v1 whole, which is shorter than its diff:
```python
import jax
import jax.numpy as jnp
from jax import lax
from jax.experimental import pallas as pl
from jax.experimental.pallas import tpu as pltpu
from jax.sharding import PartitionSpec as P

MESH = pl.DeviceIdType.MESH
F32 = jnp.float32
BF16 = jnp.bfloat16
V, CX, CY, CZ = 5, 16, 16, 256
ROWS = 1024
NDEV = 128
CAP = 16
GX, GY = 8, 16
VY = V * CY
CHUNK = 256
GROUP = 4
LIMIT = 48 * 1024 * 1024


def iota(shape, dim):
    return lax.broadcasted_iota(jnp.int32, shape, dim)


def two(a):
    hi = a.astype(BF16)
    return hi, (a - hi.astype(F32)).astype(BF16)


def dot(a, b):
    return lax.dot_general(a, b, (((1,), (0,)), ((), ())), preferred_element_type=F32)


def dot_t(a, b):
    return lax.dot_general(a, b, (((1,), (1,)), ((), ())), preferred_element_type=F32)


def flux_matrix(flux):
    col = iota((1, 256), 1)
    block = (col >= 80).astype(jnp.int32) + (col >= 160).astype(jnp.int32) + (col >= 240).astype(jnp.int32)
    side = (col >= 248).astype(jnp.int32)
    var = jnp.where(block == 3, col - 240 - 8 * side, (col >> 4) - 5 * block)
    yc = jnp.where(block == 3, 17 * side - 1, col & 15)
    y = iota((CY, 256), 0)
    here = (yc == y).astype(F32)
    back = (yc == y - 1).astype(F32)
    fwd = (yc == y + 1).astype(F32)
    mid = (block == 1).astype(F32)
    near = ((block == 1) | (block == 3)).astype(F32)
    w_mid, w_back, w_fwd = here * mid, back * near, fwd * near
    w_left, w_right = here * (block == 0).astype(F32), here * (block == 2).astype(F32)
    mains, ups, downs = [], [], []
    for a in range(V):
        row = {}
        for d in range(3):
            for s in range(2):
                total = jnp.zeros((1, 256), F32)
                for b in range(V):
                    total = jnp.where(var == b, flux[d, a, s : s + 1, b : b + 1], total)
                row[d, s] = total
        centre = (row[0, 0] - row[0, 1]) + (row[1, 0] - row[1, 1]) + (row[2, 0] - row[2, 1])
        mains.append(
            centre * w_mid - row[1, 0] * w_back + row[1, 1] * w_fwd - row[0, 0] * w_left + row[0, 1] * w_right
        )
        ups.append(row[2, 1] * w_mid)
        downs.append(row[2, 0] * w_mid)
    return jnp.concatenate(mains + ups + downs, axis=0)


def y_faces(planes):
    pad = [jnp.zeros((8 - V, CZ), F32)]
    return [jnp.concatenate([p[y : y + 1, :] for p in planes] + pad, axis=0) for y in (0, CY - 1)]


def beyond(halo_x, halo_y):
    ix, iy = lax.axis_index("gx"), lax.axis_index("gy")
    nx, ny = lax.axis_size("gx"), lax.axis_size("gy")
    keep_x = [jnp.where(ix > 0, 1.0, 0.0), jnp.where(ix < nx - 1, 1.0, 0.0)]
    keep_y = [jnp.where(iy > 0, 1.0, 0.0), jnp.where(iy < ny - 1, 1.0, 0.0)]
    ends = [two(halo_x[side] * keep_x[side]) for side in range(2)]
    rows = [
        two(jnp.concatenate([halo_y[side, x] * keep_y[side] for side in range(2)], axis=0)) for x in range(CX)
    ]
    return ends, rows


def flux_of(x, km_hi, km_lo, hi, lo, ends, rows):
    def tile(ref, part):
        left = ends[0][part] if x == 0 else ref[x - 1]
        right = ends[1][part] if x == CX - 1 else ref[x + 1]
        return jnp.concatenate([left, ref[x], right, rows[x][part]], axis=0)

    top, low = tile(hi, 0), tile(lo, 1)
    total = dot(km_hi[...], top) + dot(km_lo[...], top) + dot(km_hi[...], low)
    z = iota((VY, CZ), 1)
    fwd = jnp.where(z == CZ - 1, 0.0, pltpu.roll(total[VY : 2 * VY], CZ - 1, 1))
    back = jnp.where(z == 0, 0.0, pltpu.roll(total[2 * VY :], 1, 1))
    return total[:VY] + fwd - back


def face_copies(ix, iy, face_x, face_y, halo_x, halo_y, send, recv):
    copies = []
    for side in range(2):
        step = 2 * side - 1
        peer_x = lax.rem(ix + step + GX, GX)
        peer_y = lax.rem(iy + step + GY, GY)
        copies.append(
            pltpu.make_async_remote_copy(
                face_x.at[side], halo_x.at[1 - side], send.at[side], recv.at[side],
                device_id=(peer_x, iy), device_id_type=MESH,
            )
        )
        copies.append(
            pltpu.make_async_remote_copy(
                face_y.at[side], halo_y.at[1 - side], send.at[2 + side], recv.at[2 + side],
                device_id=(ix, peer_y), device_id_type=MESH,
            )
        )
    return copies


def ranks(onehot, onehot_b):
    before = (iota((CHUNK, CHUNK), 0) < iota((CHUNK, CHUNK), 1)).astype(F32).astype(BF16)
    ones = jnp.ones((CHUNK, CHUNK), BF16)
    carry = jnp.zeros((NDEV, CHUNK), F32)
    slots = []
    for c in range(ROWS // CHUNK):
        part = onehot_b[:, c * CHUNK : (c + 1) * CHUNK]
        rank = dot(part, before) + carry
        carry = carry + dot(part, ones)
        slots.append(jnp.sum(rank * onehot[:, c * CHUNK : (c + 1) * CHUNK], axis=0, keepdims=True))
    return slots


def hat(n, low, f):
    at = iota((n, CHUNK), 0)
    return jnp.where(at == low, 1.0 - f, jnp.where(at == low + 1, f, jnp.zeros_like(f)))


def pack(base, frac, cell, slots, onehot_b, fields):
    packed = jnp.zeros((22 * CAP, NDEV), F32)
    for c in range(ROWS // CHUNK):
        span = slice(c * CHUNK, (c + 1) * CHUNK)
        low = base[:, span]
        base_x = low // ((CZ - 1) * (CY - 1))
        rest = low - base_x * ((CZ - 1) * (CY - 1))
        base_y = rest // (CZ - 1)
        base_z = rest - base_y * (CZ - 1)
        fx, fy, fz = frac[0:1, span], frac[1:2, span], frac[2:3, span]
        z_hi, z_lo = two(hat(CZ, base_z, fz))
        w_x, w_y = hat(CX, base_x, fx), hat(CY, base_y, fy)
        w_xy = [w_x[x : x + 1] * w_y for x in range(CX)]
        right = jnp.concatenate([z_hi, z_hi, z_lo], axis=0)
        values = []
        for hi, lo in fields:
            top, rem = hi[...].reshape(CX * VY, CZ), lo[...].reshape(CX * VY, CZ)
            along = dot(jnp.concatenate([top, rem, top], axis=1), right)
            for v in range(V):
                total = jnp.zeros((CY, CHUNK), F32)
                for x in range(CX):
                    at = x * VY + v * CY
                    total = total + along[at : at + CY] * w_xy[x]
                values.append(jnp.sum(total, axis=0, keepdims=True))
        cells = cell[:, span]
        rows_hi, rows_lo = [], []
        at_slot = (iota((CAP, CHUNK), 0).astype(F32) == slots[c]).astype(F32)
        for value in values:
            hi = value.astype(BF16).astype(F32)
            rows_hi.append((at_slot * hi).astype(BF16))
            rows_lo.append((at_slot * (value - hi)).astype(BF16))
        xy = ((cells >> 8) + 1).astype(F32)
        z = (cells & 255).astype(F32)
        left = jnp.concatenate(
            rows_hi + [(at_slot * xy).astype(BF16), (at_slot * z).astype(BF16)] + rows_lo, axis=0
        )
        packed = packed + dot_t(left, onehot_b[:, span])
    half = 2 * V * CAP
    return jnp.concatenate(
        [packed[:half] + packed[half + 2 * CAP :], packed[half : half + 2 * CAP], jnp.zeros((4 * CAP, NDEV), F32)], axis=0
    )


def launch(count, flux_h, now_h, prev_h, jac_h, base_h, frac_h, dest_h, cell_h, got, start, km_hi, km_lo,
           flux, q_now, q_prev, jac, base, frac, dest, cell, now_hi, now_lo, prev_hi, prev_lo, sent, mid,
           face_x, face_y, halo_x, halo_y, load, send, recv, send_a, recv_a, send_b, recv_b):
    loads = [
        pltpu.make_async_copy(a, b, load.at[i])
        for i, (a, b) in enumerate(
            [(dest_h, dest), (flux_h, flux), (base_h, base), (frac_h, frac), (cell_h, cell),
             (prev_h, q_prev), (now_h, q_now), (jac_h, jac)]
        )
    ]
    for copy in loads:
        copy.start()
    ix, iy = lax.axis_index("gx"), lax.axis_index("gy")
    peers = [(lax.rem(ix + k, GX), iy) for k in range(1, GX)] + [(ix, lax.rem(iy + k, GY)) for k in range(1, GY)]
    barrier = pltpu.get_barrier_semaphore()
    for peer in peers:
        pl.semaphore_signal(barrier, inc=1, device_id=peer, device_id_type=MESH)

    loads[0].wait()
    live = iota((1, ROWS), 1) < count[0]
    where_to = jnp.where(live, dest[...], NDEV)
    onehot = (iota((NDEV, ROWS), 0) == where_to).astype(F32)
    onehot_b = onehot.astype(BF16)
    slots = ranks(onehot, onehot_b)
    for copy in loads[1:]:
        copy.wait()
    for x in range(CX):
        for v in range(V):
            for ref, top, low in ((q_prev, prev_hi, prev_lo), (q_now, now_hi, now_lo)):
                hi, lo = two(ref[v, x])
                top[x, v * CY : (v + 1) * CY, :] = hi
                low[x, v * CY : (v + 1) * CY, :] = lo
        lo_y, hi_y = y_faces([q_now[v, x] for v in range(V)])
        face_y[0, x] = lo_y
        face_y[1, x] = hi_y
    for v in range(V):
        face_x[0, v * CY : (v + 1) * CY, :] = q_now[v, 0]
        face_x[1, v * CY : (v + 1) * CY, :] = q_now[v, CX - 1]
    full = pack(base, frac, cell, slots, onehot_b, ((prev_hi, prev_lo), (now_hi, now_lo)))
    for h in range(2):
        sent[:, :, h, :] = full[h * 128 : (h + 1) * 128].T.reshape(GX, GY, 128)

    pl.semaphore_wait(barrier, len(peers))
    along = []
    for k in range(1, GX):
        to = lax.rem(ix + k, GX)
        copy = pltpu.make_async_remote_copy(
            sent.at[to], mid.at[ix], send_a.at[k - 1], recv_a.at[k - 1], device_id=(to, iy), device_id_type=MESH
        )
        copy.start()
        along.append(copy)
    faces = face_copies(ix, iy, face_x, face_y, halo_x, halo_y, send, recv)
    for copy in faces:
        copy.start()
    mid[ix] = sent[ix]
    hi, lo = two(flux_matrix(flux))
    km_hi[...] = hi
    km_lo[...] = lo
    for copy in along:
        copy.wait_recv()
    across = []
    for k in range(1, GY):
        to = lax.rem(iy + k, GY)
        copy = pltpu.make_async_remote_copy(
            mid.at[:, to], got.at[iy], send_b.at[k - 1], recv_b.at[k - 1], device_id=(ix, to), device_id_type=MESH
        )
        copy.start()
        across.append(copy)
    got[iy] = mid[:, iy]
    for copy in along:
        copy.wait_send()
    for copy in faces:
        copy.wait()
    ends, rows = beyond(halo_x, halo_y)
    for x in range(CX):
        flux_x = flux_of(x, km_hi, km_lo, now_hi, now_lo, ends, rows)
        scale = 0.2 * jac[x]
        for v in range(V):
            part = slice(v * CY, (v + 1) * CY)
            start[x, part, :] = q_now[v, x] - scale * (flux_x[part] + (q_prev[v, x] - q_now[v, x]))
    for copy in across:
        copy.wait()


def settle(got, start, q_now, q_prev, jac, later, hi_out, lo_out, halo_x, halo_y,
           face_x, face_y, parts, places, at_z, send, recv):
    ix, iy = lax.axis_index("gx"), lax.axis_index("gy")
    barrier = pltpu.get_barrier_semaphore()
    for step in (-1, 1):
        for peer in ((lax.rem(ix + step + GX, GX), iy), (ix, lax.rem(iy + step + GY, GY))):
            pl.semaphore_signal(barrier, inc=1, device_id=peer, device_id_type=MESH)

    halves = [got[:, :, h, :].reshape(NDEV, 128) for h in range(2)]
    turned = jnp.concatenate([h.T for h in halves], axis=0)
    for s in range(CAP):
        lanes = slice(s * NDEV, (s + 1) * NDEV)
        for g in range(2):
            for v in range(V):
                row = turned[(g * V + v) * CAP + s :][:1]
                hi, lo = two(jnp.broadcast_to(row, (CY, NDEV)))
                parts[g * 11 + v, :, lanes] = hi
                parts[g * 11 + V + v, :, lanes] = lo
        parts[10, :, lanes] = jnp.ones((CY, NDEV), BF16)
        places[:, lanes] = jnp.broadcast_to(turned[10 * CAP + s :][:1], (CY, NDEV))
        column = halves[1][:, 3 * CAP + s : 3 * CAP + s + 1]
        at_z[lanes, :] = (iota((NDEV, CZ), 1).astype(F32) == column).astype(F32).astype(BF16)

    def landing(group, first, last):
        left = []
        for j in range(GROUP):
            mark = (iota((CY, 1), 0) + ((group * GROUP + j) * CY + 1)).astype(F32)
            here = (places[...] == mark).astype(F32).astype(BF16)
            left += [parts[i] * here for i in range(first, last)]
        return dot(jnp.concatenate(left, axis=0), at_z[...])

    def rows_of(landed, j, n, i):
        return landed[(j * n + i) * CY : (j * n + i + 1) * CY]

    for group in range(CX // GROUP):
        landed = landing(group, 0, 11)
        for j in range(GROUP):
            x = group * GROUP + j
            scale = 0.2 * jac[x]
            hits = rows_of(landed, j, 11, 10)
            fresh = []
            for v in range(V):
                part = slice(v * CY, (v + 1) * CY)
                q, qp = q_now[v, x], q_prev[v, x]
                target = rows_of(landed, j, 11, v) + rows_of(landed, j, 11, V + v)
                w = start[x, part, :] - scale * (2.0 * (hits * q - target))
                hi, lo = two(w)
                hi_out[x, part, :] = hi
                lo_out[x, part, :] = lo
                later[x, part, :] = w - scale * ((3.0 * w - 4.0 * q + qp) + 2.0 * (hits * w))
                fresh.append(w)
                if x in (0, CX - 1):
                    face_x[0 if x == 0 else 1, part, :] = w
            lo_y, hi_y = y_faces(fresh)
            face_y[0, x] = lo_y
            face_y[1, x] = hi_y
    pl.semaphore_wait(barrier, 4)
    faces = face_copies(ix, iy, face_x, face_y, halo_x, halo_y, send, recv)
    for copy in faces:
        copy.start()
    for group in range(CX // GROUP):
        landed = landing(group, 11, 21)
        for j in range(GROUP):
            x = group * GROUP + j
            scale = 0.4 * jac[x]
            for v in range(V):
                part = slice(v * CY, (v + 1) * CY)
                target = rows_of(landed, j, 10, v) + rows_of(landed, j, 10, V + v)
                later[x, part, :] = later[x, part, :] + scale * target
    for copy in faces:
        copy.wait()


def second(hi, lo, later, jac, halo_x, halo_y, km_hi, km_lo, out):
    ends, rows = beyond(halo_x, halo_y)
    for x in range(CX):
        flux = flux_of(x, km_hi, km_lo, hi, lo, ends, rows)
        scale = 0.2 * jac[x]
        for v in range(V):
            part = slice(v * CY, (v + 1) * CY)
            out[v, x] = later[x, part, :] - scale * flux[part]


VM = pl.BlockSpec(memory_space=pltpu.VMEM)
SM = pl.BlockSpec(memory_space=pltpu.SMEM)
HB = pl.BlockSpec(memory_space=pltpu.HBM)
FACES = [((2, VY, CZ), F32), ((2, CX, 8, CZ), F32)]
PLANES = ((CX, VY, CZ), F32)
PARTS = [((CX, VY, CZ), BF16)] * 2
MATRIX = [((3 * VY, 256), BF16)] * 2


def shapes(entries):
    return [jax.ShapeDtypeStruct(*e) for e in entries]


def vmem(entries):
    return [pltpu.VMEM(*e) for e in entries]


def call_launch(count, flux, q_now, q_prev, jac, base, frac, dest, cell):
    ins = [flux, q_now, q_prev, jac, base, frac, dest, cell]
    return pl.pallas_call(
        launch,
        out_shape=shapes([((GY, GX, 2, 128), F32), PLANES] + MATRIX),
        in_specs=[SM] + [HB] * 8,
        out_specs=[VM] * 4,
        scratch_shapes=vmem([(a.shape, a.dtype) for a in ins])
        + vmem(PARTS * 2 + [((GX, GY, 2, 128), F32)] * 2 + FACES * 2)
        + [pltpu.SemaphoreType.DMA((8,))]
        + [pltpu.SemaphoreType.DMA((4,))] * 2
        + [pltpu.SemaphoreType.DMA((GX - 1,))] * 2
        + [pltpu.SemaphoreType.DMA((GY - 1,))] * 2,
        compiler_params=pltpu.CompilerParams(vmem_limit_bytes=LIMIT, collective_id=0, has_side_effects=True),
        name="launch",
    )(count, *ins)


def call_settle(got, start, q_now, q_prev, jac):
    return pl.pallas_call(
        settle,
        out_shape=shapes([PLANES] + PARTS + FACES),
        in_specs=[VM] * 5,
        out_specs=[VM] * 5,
        scratch_shapes=vmem(
            FACES + [((21, CY, NDEV * CAP), BF16), ((CY, NDEV * CAP), F32), ((NDEV * CAP, CZ), BF16)]
        )
        + [pltpu.SemaphoreType.DMA((4,))] * 2,
        compiler_params=pltpu.CompilerParams(vmem_limit_bytes=LIMIT, collective_id=1, has_side_effects=True),
        name="settle",
    )(got, start, q_now, q_prev, jac)


def call_second(hi, lo, later, jac, halo_x, halo_y, km_hi, km_lo):
    return pl.pallas_call(
        second,
        out_shape=jax.ShapeDtypeStruct((V, CX, CY, CZ), F32),
        in_specs=[VM] * 8,
        out_specs=VM,
        compiler_params=pltpu.CompilerParams(vmem_limit_bytes=LIMIT),
        name="second",
    )(hi, lo, later, jac, halo_x, halo_y, km_hi, km_lo)


def body(q_now, q_prev, jacobian, flux_split, donor_base, donor_frac, fringe_dest, receptor_cell, fringe_count):
    got, start, km_hi, km_lo = call_launch(
        fringe_count, flux_split.transpose(0, 2, 1, 3), q_now, q_prev, jacobian, donor_base.reshape(1, ROWS),
        donor_frac, fringe_dest.reshape(1, ROWS), receptor_cell.reshape(1, ROWS),
    )
    later, hi, lo, halo_x, halo_y = call_settle(got, start, q_now, q_prev, jacobian)
    return call_second(hi, lo, later, jacobian, halo_x, halo_y, km_hi, km_lo)


def solution(mesh):
    return jax.shard_map(
        body,
        mesh=mesh,
        in_specs=(
            P(None, "gx", "gy", None),
            P(None, "gx", "gy", None),
            P("gx", "gy", None),
            P(),
            P(("gx", "gy")),
            P(None, ("gx", "gy")),
            P(("gx", "gy"), None),
            P(("gx", "gy")),
            P(("gx", "gy")),
        ),
        out_specs=P(None, "gx", "gy", None),
        check_vma=False,
    )
```

time: 62 us -> 42.9 us (0.69)
  Pallas kernels: 54.7 us -> 34.7 us
  local copies, waits for them, and re-layouts: 6.24 us -> 7.07 us
    pallas_call x4 -> x2, Pallas kernels: 47.9 us -> 31.8 us  [the longest x1 20.9 us: call_launch(): pl.pallas_call(launch, out_shape=shapes([((GY, GX, 2, 128), F32), PLANES]...]
    pallas_call x1, Pallas kernels: 6.75 us -> 2.9 us  [call_second(): pl.pallas_call(second, out_shape=jax.ShapeDtypeStruct((V, CX, CY, CZ), F3...]
    unnamed x17 -> x20, local copies, waits for them, and re-layouts: 6.13 us -> 7.07 us
where the time goes in v1:
time: 42.9 us; the launch traced here: 42.5 us
  Pallas kernels  34.7 us (81%)
  local copies, waits for them, and re-layouts  7.07 us (16%)
  between operations  0.7 us (2%)
    pallas_call x1, Pallas kernels, call_launch(): pl.pallas_call(launch, out_shape=shapes([((GY, GX, 2, 128), F32), PLANES]...  20.9 us
    pallas_call x1, Pallas kernels, call_settle(): pl.pallas_call(settle, out_shape=shapes([PLANES] + PARTS + FACES), in_spe...  10.9 us
    unnamed x20, local copies, waits for them, and re-layouts  7.07 us
    pallas_call x1, Pallas kernels, call_second(): pl.pallas_call(second, out_shape=jax.ShapeDtypeStruct((V, CX, CY, CZ), F3...  2.9 us

profile of v1, /device:TPU:0, one launch (start us, length us, event | category | flops | bytes accessed | tf_op | source)
XLA Modules:
  0.0 42.5 jit_solution(12722442349184970046)
XLA Ops:
  0.7 0.0 copy-start
  0.7 1.3 %copy-done = f32[5,16,16,256]{3,2,1,0:T(8,128)S(1)} copy-done((f32[5,16,16,256]{3,2,1,0:T(8,128)S(1)}, f32[5,16,16,256]{3,2,1,0:T(8,128)}, u32[]{:S(2)}) %copy-start) | copy-done | bytes 1310744
  2.0 0.0 copy-start.2
  2.0 1.3 %copy-done.2 = f32[5,16,16,256]{3,2,1,0:T(8,128)S(1)} copy-done((f32[5,16,16,256]{3,2,1,0:T(8,128)S(1)}, f32[5,16,16,256]{3,2,1,0:T(8,128)}, u32[]{:S(2)}) %copy-start.2) | copy-done | bytes 1310744
  3.3 0.0 copy-start.3
  3.3 0.9 %copy-done.3 = f32[16,16,256]{2,1,0:T(8,128)S(1)} copy-done((f32[16,16,256]{2,1,0:T(8,128)S(1)}, f32[16,16,256]{2,1,0:T(8,128)}, u32[]{:S(2)}) %copy-start.3) | copy-done | bytes 262168
  4.2 0.0 copy-start.5
  4.2 0.7 %copy-done.5 = f32[3,1024]{1,0:T(4,128)S(1)} copy-done((f32[3,1024]{1,0:T(4,128)S(1)}, f32[3,1024]{1,0:T(4,128)}, u32[]{:S(2)}) %copy-start.5) | copy-done | bytes 12312
  5.0 0.0 copy-start.6
  5.0 0.7 %copy-done.6 = f32[3,2,5,5]{3,1,2,0:T(2,128)S(1)} copy-done((f32[3,2,5,5]{3,1,2,0:T(2,128)S(1)}, f32[3,2,5,5]{3,1,2,0:T(2,128)}, u32[]{:S(2)}) %copy-start.6) | copy-done | bytes 624
  5.7 0.0 copy-start.7
  5.7 0.7 %copy-done.7 = s32[1024]{0:T(1024)S(1)} copy-done((s32[1024]{0:T(1024)S(1)}, s32[1024]{0:T(1024)}, u32[]{:S(2)}) %copy-start.7) | copy-done | bytes 4120
  6.4 0.0 copy-start.8
  6.4 0.7 %copy-done.8 = s32[1024,1]{0,1:T(1,128)S(1)} copy-done((s32[1024,1]{0,1:T(1,128)S(1)}, s32[1024,1]{0,1:T(1,128)}, u32[]{:S(2)}) %copy-start.8) | copy-done | bytes 4120
  7.0 0.0 copy-start.9
  7.0 0.7 %copy-done.9 = s32[1024]{0:T(1024)S(1)} copy-done((s32[1024]{0:T(1024)S(1)}, s32[1024]{0:T(1024)}, u32[]{:S(2)}) %copy-start.9) | copy-done | bytes 4120
  7.7 0.0 copy-start.1
  7.7 0.0 copy-start.4
  7.7 20.9 %launch.1 = (f32[16,8,2,128]{3,2,1,0:T(2,128)S(1)}, f32[16,80,256]{2,1,0:T(8,128)S(1)}, bf16[240,256]{1,0:T(8,128)(2,1)S(1)}, bf16[240,256]{1,0:T(8,128)(2,1)S(1)}) custom-call(s32[1]{0:T(128)S(6)} %copy.10.count, f32[3,5,2,5]{3,2,1,0:T(2,128)S(1)} %bitcast.4, f32[5,16,16,256]{3,2,1,0:T(8,128)S(1)} %copy-done, f32[5,16,16,256]{3,2,1,0:T(8,128)S(1)} %copy-done.2, ...), custom_call_target="tpu_custom_call" | custom-call | tf_op jit(solution)/shard_map/launch/pallas_call | solution.py:370
  28.6 0.0 copy-done.1
  28.6 0.0 copy-done.4
  28.7 10.9 %settle.1 = (f32[16,80,256]{2,1,0:T(8,128)S(1)}, bf16[16,80,256]{2,1,0:T(8,128)(2,1)S(1)}, bf16[16,80,256]{2,1,0:T(8,128)(2,1)S(1)}, f32[2,80,256]{2,1,0:T(8,128)S(1)}, f32[2,16,8,256]{3,2,1,0:T(8,128)S(1)}) custom-call(f32[16,8,2,128]{3,2,1,0:T(2,128)S(1)} %get-tuple-element.14.got, f32[16,80,256]{2,1,0:T(8,128)S(1)} %get-tuple-element.15.start, ...), custom_call_target="tpu_custom_call" | custom-call | tf_op jit(solution)/shard_map/settle/pallas_call | solution.py:387
  39.6 2.9 %second.1 = f32[5,16,16,256]{3,2,1,0:T(8,128)} custom-call(bf16[16,80,256]{2,1,0:T(8,128)(2,1)S(1)} %get-tuple-element.16.hi, bf16[16,80,256]{2,1,0:T(8,128)(2,1)S(1)} %get-tuple-element.17.lo, f32[16,80,256]{2,1,0:T(8,128)S(1)} %get-tuple-element.18.later, f32[16,16,256]{2,1,0:T(8,128)S(1)} %copy-done.4, f32[2,80,256]{2,1,0:T(8,128)S(1)} %get-tuple-element.19.halo_x, ...), custom_call_target="tpu_custom_call" | custom-call | tf_op jit(solution)/shard_map/second/pallas_call | solution.py:402
Async XLA Ops:
  0.7 1.3 %copy-start = (f32[5,16,16,256]{3,2,1,0:T(8,128)S(1)}, f32[5,16,16,256]{3,2,1,0:T(8,128)}, u32[]{:S(2)}) copy-start(f32[5,16,16,256]{3,2,1,0:T(8,128)} %q_now.1) | copy-start | bytes 3932164
  2.0 1.3 %copy-start.2 = (f32[5,16,16,256]{3,2,1,0:T(8,128)S(1)}, f32[5,16,16,256]{3,2,1,0:T(8,128)}, u32[]{:S(2)}) copy-start(f32[5,16,16,256]{3,2,1,0:T(8,128)} %q_prev.1) | copy-start | bytes 3932164
  3.3 0.9 %copy-start.3 = (f32[16,16,256]{2,1,0:T(8,128)S(1)}, f32[16,16,256]{2,1,0:T(8,128)}, u32[]{:S(2)}) copy-start(f32[16,16,256]{2,1,0:T(8,128)} %jac.3) | copy-start | bytes 786436
  4.2 0.7 %copy-start.5 = (f32[3,1024]{1,0:T(4,128)S(1)}, f32[3,1024]{1,0:T(4,128)}, u32[]{:S(2)}) copy-start(f32[3,1024]{1,0:T(4,128)} %frac_h.1) | copy-start | bytes 36868
  5.0 0.7 %copy-start.6 = (f32[3,2,5,5]{3,1,2,0:T(2,128)S(1)}, f32[3,2,5,5]{3,1,2,0:T(2,128)}, u32[]{:S(2)}) copy-start(f32[3,2,5,5]{3,1,2,0:T(2,128)} %param.12) | copy-start | bytes 1804
  5.7 0.7 %copy-start.7 = (s32[1024]{0:T(1024)S(1)}, s32[1024]{0:T(1024)}, u32[]{:S(2)}) copy-start(s32[1024]{0:T(1024)} %param.13) | copy-start | bytes 12292
  6.4 0.7 %copy-start.8 = (s32[1024,1]{0,1:T(1,128)S(1)}, s32[1024,1]{0,1:T(1,128)}, u32[]{:S(2)}) copy-start(s32[1024,1]{0,1:T(1,128)} %param.15) | copy-start | bytes 12292
  7.0 0.7 %copy-start.9 = (s32[1024]{0:T(1024)S(1)}, s32[1024]{0:T(1024)}, u32[]{:S(2)}) copy-start(s32[1024]{0:T(1024)} %param.16) | copy-start | bytes 12292
  7.7 20.9 %copy-start.1 = (f32[5,16,16,256]{3,2,1,0:T(8,128)S(1)}, f32[5,16,16,256]{3,2,1,0:T(8,128)}, u32[]{:S(2)}) copy-start(f32[5,16,16,256]{3,2,1,0:T(8,128)} %q_now.1) | copy-start | bytes 3932164
  7.7 20.9 %copy-start.4 = (f32[16,16,256]{2,1,0:T(8,128)S(1)}, f32[16,16,256]{2,1,0:T(8,128)}, u32[]{:S(2)}) copy-start(f32[16,16,256]{2,1,0:T(8,128)} %jac.3) | copy-start | bytes 786436

commit v2 on v1

--- a/solution.py
+++ b/solution.py
@@ -138,8 +138,7 @@
     return jnp.where(at == low, 1.0 - f, jnp.where(at == low + 1, f, jnp.zeros_like(f)))
 
 
-def pack(base, frac, cell, slots, onehot_b, fields):
-    packed = jnp.zeros((22 * CAP, NDEV), F32)
+def stencils(base, frac, z_parts, w_xy):
     for c in range(ROWS // CHUNK):
         span = slice(c * CHUNK, (c + 1) * CHUNK)
         low = base[:, span]
@@ -148,47 +147,49 @@
         base_y = rest // (CZ - 1)
         base_z = rest - base_y * (CZ - 1)
         fx, fy, fz = frac[0:1, span], frac[1:2, span], frac[2:3, span]
-        z_hi, z_lo = two(hat(CZ, base_z, fz))
+        hi, lo = two(hat(CZ, base_z, fz))
+        z_parts[c, 0:CZ, :] = hi
+        z_parts[c, CZ : 2 * CZ, :] = hi
+        z_parts[c, 2 * CZ :, :] = lo
         w_x, w_y = hat(CX, base_x, fx), hat(CY, base_y, fy)
-        w_xy = [w_x[x : x + 1] * w_y for x in range(CX)]
-        right = jnp.concatenate([z_hi, z_hi, z_lo], axis=0)
-        values = []
-        for hi, lo in fields:
-            top, rem = hi[...].reshape(CX * VY, CZ), lo[...].reshape(CX * VY, CZ)
-            along = dot(jnp.concatenate([top, rem, top], axis=1), right)
-            for v in range(V):
-                total = jnp.zeros((CY, CHUNK), F32)
-                for x in range(CX):
-                    at = x * VY + v * CY
-                    total = total + along[at : at + CY] * w_xy[x]
-                values.append(jnp.sum(total, axis=0, keepdims=True))
-        cells = cell[:, span]
-        rows_hi, rows_lo = [], []
-        at_slot = (iota((CAP, CHUNK), 0).astype(F32) == slots[c]).astype(F32)
-        for value in values:
-            hi = value.astype(BF16).astype(F32)
-            rows_hi.append((at_slot * hi).astype(BF16))
-            rows_lo.append((at_slot * (value - hi)).astype(BF16))
-        xy = ((cells >> 8) + 1).astype(F32)
-        z = (cells & 255).astype(F32)
-        left = jnp.concatenate(
-            rows_hi + [(at_slot * xy).astype(BF16), (at_slot * z).astype(BF16)] + rows_lo, axis=0
-        )
-        packed = packed + dot_t(left, onehot_b[:, span])
-    half = 2 * V * CAP
-    return jnp.concatenate(
-        [packed[:half] + packed[half + 2 * CAP :], packed[half : half + 2 * CAP], jnp.zeros((4 * CAP, NDEV), F32)], axis=0
-    )
-
-
-def launch(count, flux_h, now_h, prev_h, jac_h, base_h, frac_h, dest_h, cell_h, got, start, km_hi, km_lo,
-           flux, q_now, q_prev, jac, base, frac, dest, cell, now_hi, now_lo, prev_hi, prev_lo, sent, mid,
-           face_x, face_y, halo_x, halo_y, load, send, recv, send_a, recv_a, send_b, recv_b):
+        for x in range(CX):
+            w_xy[c, x] = w_x[x : x + 1] * w_y
+
+
+def donate(c, hi, lo, z_parts, w_xy, slots, onehot_b, extra):
+    top, rem = hi[...].reshape(CX * VY, CZ), lo[...].reshape(CX * VY, CZ)
+    along = dot(jnp.concatenate([top, rem, top], axis=1), z_parts[c])
+    at_slot = (iota((CAP, CHUNK), 0).astype(F32) == slots[c]).astype(F32)
+    rows_hi, rows_lo = [], []
+    for v in range(V):
+        total = jnp.zeros((CY, CHUNK), F32)
+        for x in range(CX):
+            at = x * VY + v * CY
+            total = total + along[at : at + CY] * w_xy[c, x]
+        value = jnp.sum(total, axis=0, keepdims=True)
+        first = value.astype(BF16).astype(F32)
+        rows_hi.append((at_slot * first).astype(BF16))
+        rows_lo.append((at_slot * (value - first)).astype(BF16))
+    rows_hi += [(at_slot * part.astype(F32)).astype(BF16) for part in extra]
+    return dot_t(jnp.concatenate(rows_hi + rows_lo, axis=0), onehot_b[:, c * CHUNK : (c + 1) * CHUNK])
+
+
+def by_block(packed, extra):
+    n, m = V * CAP, (V + extra) * CAP
+    rows = [packed[:n] + packed[m:]] + ([packed[n:m]] if extra else []) + [jnp.zeros((128 - m, NDEV), F32)]
+    return jnp.concatenate(rows, axis=0).T.reshape(GX, GY, 128)
+
+
+def advance(count, flux_h, now_h, prev_h, jac_h, base_h, frac_h, dest_h, cell_h,
+            later, hi_out, lo_out, halo2_x, halo2_y, km_hi, km_lo,
+            flux, q_now, q_prev, jac, base, frac, dest, cell, now_hi, now_lo, prev_hi, prev_lo, start, z_parts, w_xy,
+            sent, mid, got, face_x, face_y, halo_x, halo_y, face2_x, face2_y, parts, places, at_z,
+            load, send, recv, send2, recv2, send_a, recv_a, send_b, recv_b):
     loads = [
         pltpu.make_async_copy(a, b, load.at[i])
         for i, (a, b) in enumerate(
-            [(dest_h, dest), (flux_h, flux), (base_h, base), (frac_h, frac), (cell_h, cell),
-             (prev_h, q_prev), (now_h, q_now), (jac_h, jac)]
+            [(dest_h, dest), (base_h, base), (frac_h, frac), (prev_h, q_prev), (now_h, q_now), (cell_h, cell),
+             (flux_h, flux), (jac_h, jac)]
         )
     ]
     for copy in loads:
@@ -199,59 +200,90 @@
     for peer in peers:
         pl.semaphore_signal(barrier, inc=1, device_id=peer, device_id_type=MESH)
 
-    loads[0].wait()
+    def along_gx(wave):
+        copies = []
+        for k in range(1, GX):
+            to = lax.rem(ix + k, GX)
+            copies.append(
+                pltpu.make_async_remote_copy(
+                    sent.at[wave, to], mid.at[wave, ix], send_a.at[wave, k - 1], recv_a.at[wave, k - 1],
+                    device_id=(to, iy), device_id_type=MESH,
+                )
+            )
+        for copy in copies:
+            copy.start()
+        mid[wave, ix] = sent[wave, ix]
+        return copies
+
+    def along_gy(wave):
+        copies = []
+        for k in range(1, GY):
+            to = lax.rem(iy + k, GY)
+            copies.append(
+                pltpu.make_async_remote_copy(
+                    mid.at[wave, :, to], got.at[wave, iy], send_b.at[wave, k - 1], recv_b.at[wave, k - 1],
+                    device_id=(ix, to), device_id_type=MESH,
+                )
+            )
+        for copy in copies:
+            copy.start()
+        got[wave, iy] = mid[wave, :, iy]
+        return copies
+
+    for copy in loads[:3]:
+        copy.wait()
     live = iota((1, ROWS), 1) < count[0]
     where_to = jnp.where(live, dest[...], NDEV)
     onehot = (iota((NDEV, ROWS), 0) == where_to).astype(F32)
     onehot_b = onehot.astype(BF16)
     slots = ranks(onehot, onehot_b)
-    for copy in loads[1:]:
-        copy.wait()
+    stencils(base, frac, z_parts, w_xy)
+    loads[3].wait()
+    loads[5].wait()
     for x in range(CX):
         for v in range(V):
-            for ref, top, low in ((q_prev, prev_hi, prev_lo), (q_now, now_hi, now_lo)):
-                hi, lo = two(ref[v, x])
-                top[x, v * CY : (v + 1) * CY, :] = hi
-                low[x, v * CY : (v + 1) * CY, :] = lo
+            hi, lo = two(q_prev[v, x])
+            prev_hi[x, v * CY : (v + 1) * CY, :] = hi
+            prev_lo[x, v * CY : (v + 1) * CY, :] = lo
+    packed = jnp.zeros((12 * CAP, NDEV), F32)
+    for c in range(ROWS // CHUNK):
+        cells = cell[:, c * CHUNK : (c + 1) * CHUNK]
+        packed = packed + donate(
+            c, prev_hi, prev_lo, z_parts, w_xy, slots, onehot_b, ((cells >> 8) + 1, cells & 255)
+        )
+    sent[0, :, :, 0, :] = by_block(packed, 2)
+
+    pl.semaphore_wait(barrier, len(peers))
+    first_a = along_gx(0)
+    for i in (4, 6, 7):
+        loads[i].wait()
+    for x in range(CX):
+        for v in range(V):
+            hi, lo = two(q_now[v, x])
+            now_hi[x, v * CY : (v + 1) * CY, :] = hi
+            now_lo[x, v * CY : (v + 1) * CY, :] = lo
         lo_y, hi_y = y_faces([q_now[v, x] for v in range(V)])
         face_y[0, x] = lo_y
         face_y[1, x] = hi_y
     for v in range(V):
         face_x[0, v * CY : (v + 1) * CY, :] = q_now[v, 0]
         face_x[1, v * CY : (v + 1) * CY, :] = q_now[v, CX - 1]
-    full = pack(base, frac, cell, slots, onehot_b, ((prev_hi, prev_lo), (now_hi, now_lo)))
-    for h in range(2):
-        sent[:, :, h, :] = full[h * 128 : (h + 1) * 128].T.reshape(GX, GY, 128)
-
-    pl.semaphore_wait(barrier, len(peers))
-    along = []
-    for k in range(1, GX):
-        to = lax.rem(ix + k, GX)
-        copy = pltpu.make_async_remote_copy(
-            sent.at[to], mid.at[ix], send_a.at[k - 1], recv_a.at[k - 1], device_id=(to, iy), device_id_type=MESH
-        )
-        copy.start()
-        along.append(copy)
     faces = face_copies(ix, iy, face_x, face_y, halo_x, halo_y, send, recv)
     for copy in faces:
         copy.start()
-    mid[ix] = sent[ix]
+    packed = jnp.zeros((10 * CAP, NDEV), F32)
+    for c in range(0, 2):
+        packed = packed + donate(c, now_hi, now_lo, z_parts, w_xy, slots, onehot_b, ())
+    for copy in first_a:
+        copy.wait_recv()
+    first_b = along_gy(0)
+    for c in range(2, 4):
+        packed = packed + donate(c, now_hi, now_lo, z_parts, w_xy, slots, onehot_b, ())
+    sent[1, :, :, 0, :] = by_block(packed, 0)
+    second_a = along_gx(1)
     hi, lo = two(flux_matrix(flux))
     km_hi[...] = hi
     km_lo[...] = lo
-    for copy in along:
-        copy.wait_recv()
-    across = []
-    for k in range(1, GY):
-        to = lax.rem(iy + k, GY)
-        copy = pltpu.make_async_remote_copy(
-            mid.at[:, to], got.at[iy], send_b.at[k - 1], recv_b.at[k - 1], device_id=(ix, to), device_id_type=MESH
-        )
-        copy.start()
-        across.append(copy)
-    got[iy] = mid[:, iy]
-    for copy in along:
-        copy.wait_send()
     for copy in faces:
         copy.wait()
     ends, rows = beyond(halo_x, halo_y)
@@ -261,31 +293,29 @@
         for v in range(V):
             part = slice(v * CY, (v + 1) * CY)
             start[x, part, :] = q_now[v, x] - scale * (flux_x[part] + (q_prev[v, x] - q_now[v, x]))
-    for copy in across:
-        copy.wait()
-
-
-def settle(got, start, q_now, q_prev, jac, later, hi_out, lo_out, halo_x, halo_y,
-           face_x, face_y, parts, places, at_z, send, recv):
-    ix, iy = lax.axis_index("gx"), lax.axis_index("gy")
-    barrier = pltpu.get_barrier_semaphore()
-    for step in (-1, 1):
-        for peer in ((lax.rem(ix + step + GX, GX), iy), (ix, lax.rem(iy + step + GY, GY))):
-            pl.semaphore_signal(barrier, inc=1, device_id=peer, device_id_type=MESH)
-
-    halves = [got[:, :, h, :].reshape(NDEV, 128) for h in range(2)]
-    turned = jnp.concatenate([h.T for h in halves], axis=0)
+    for copy in second_a:
+        copy.wait_recv()
+    second_b = along_gy(1)
+    for copy in first_b:
+        copy.wait_recv()
+
+    def spread(wave):
+        rows = got[wave, :, :, 0, :].reshape(NDEV, 128)
+        turned = rows.T
+        for s in range(CAP):
+            lanes = slice(s * NDEV, (s + 1) * NDEV)
+            for v in range(V):
+                hi, lo = two(jnp.broadcast_to(turned[v * CAP + s :][:1], (CY, NDEV)))
+                parts[wave * 11 + v, :, lanes] = hi
+                parts[wave * 11 + V + v, :, lanes] = lo
+        return rows, turned
+
+    rows, turned = spread(0)
+    parts[10] = jnp.ones((CY, NDEV * CAP), BF16)
     for s in range(CAP):
         lanes = slice(s * NDEV, (s + 1) * NDEV)
-        for g in range(2):
-            for v in range(V):
-                row = turned[(g * V + v) * CAP + s :][:1]
-                hi, lo = two(jnp.broadcast_to(row, (CY, NDEV)))
-                parts[g * 11 + v, :, lanes] = hi
-                parts[g * 11 + V + v, :, lanes] = lo
-        parts[10, :, lanes] = jnp.ones((CY, NDEV), BF16)
-        places[:, lanes] = jnp.broadcast_to(turned[10 * CAP + s :][:1], (CY, NDEV))
-        column = halves[1][:, 3 * CAP + s : 3 * CAP + s + 1]
+        places[:, lanes] = jnp.broadcast_to(turned[5 * CAP + s :][:1], (CY, NDEV))
+        column = rows[:, 6 * CAP + s : 6 * CAP + s + 1]
         at_z[lanes, :] = (iota((NDEV, CZ), 1).astype(F32) == column).astype(F32).astype(BF16)
 
     def landing(group, first, last):
@@ -317,14 +347,16 @@
                 later[x, part, :] = w - scale * ((3.0 * w - 4.0 * q + qp) + 2.0 * (hits * w))
                 fresh.append(w)
                 if x in (0, CX - 1):
-                    face_x[0 if x == 0 else 1, part, :] = w
+                    face2_x[0 if x == 0 else 1, part, :] = w
             lo_y, hi_y = y_faces(fresh)
-            face_y[0, x] = lo_y
-            face_y[1, x] = hi_y
-    pl.semaphore_wait(barrier, 4)
-    faces = face_copies(ix, iy, face_x, face_y, halo_x, halo_y, send, recv)
-    for copy in faces:
+            face2_y[0, x] = lo_y
+            face2_y[1, x] = hi_y
+    faces2 = face_copies(ix, iy, face2_x, face2_y, halo2_x, halo2_y, send2, recv2)
+    for copy in faces2:
         copy.start()
+    for copy in second_b:
+        copy.wait_recv()
+    spread(1)
     for group in range(CX // GROUP):
         landed = landing(group, 11, 21)
         for j in range(GROUP):
@@ -334,7 +366,9 @@
                 part = slice(v * CY, (v + 1) * CY)
                 target = rows_of(landed, j, 10, v) + rows_of(landed, j, 10, V + v)
                 later[x, part, :] = later[x, part, :] + scale * target
-    for copy in faces:
+    for copy in first_a + first_b + second_a + second_b:
+        copy.wait_send()
+    for copy in faces2:
         copy.wait()
 
 
@@ -365,37 +399,22 @@
     return [pltpu.VMEM(*e) for e in entries]
 
 
-def call_launch(count, flux, q_now, q_prev, jac, base, frac, dest, cell):
-    ins = [flux, q_now, q_prev, jac, base, frac, dest, cell]
+def call_advance(count, flux, q_now, q_prev, jac, base, frac, dest, cell):
+    ins = [pltpu.with_memory_space_constraint(a, pltpu.HBM) for a in (flux, q_now, q_prev, jac, base, frac, dest, cell)]
+    dma = pltpu.SemaphoreType.DMA
     return pl.pallas_call(
-        launch,
-        out_shape=shapes([((GY, GX, 2, 128), F32), PLANES] + MATRIX),
+        advance,
+        out_shape=shapes([PLANES] + PARTS + FACES + MATRIX),
         in_specs=[SM] + [HB] * 8,
-        out_specs=[VM] * 4,
+        out_specs=[VM] * 7,
         scratch_shapes=vmem([(a.shape, a.dtype) for a in ins])
-        + vmem(PARTS * 2 + [((GX, GY, 2, 128), F32)] * 2 + FACES * 2)
-        + [pltpu.SemaphoreType.DMA((8,))]
-        + [pltpu.SemaphoreType.DMA((4,))] * 2
-        + [pltpu.SemaphoreType.DMA((GX - 1,))] * 2
-        + [pltpu.SemaphoreType.DMA((GY - 1,))] * 2,
+        + vmem(PARTS * 2 + [PLANES, ((4, 3 * CZ, CHUNK), BF16), ((4, CX, CY, CHUNK), F32)])
+        + vmem([((2, GX, GY, 1, 128), F32)] * 2 + [((2, GY, GX, 1, 128), F32)] + FACES * 3)
+        + vmem([((21, CY, NDEV * CAP), BF16), ((CY, NDEV * CAP), F32), ((NDEV * CAP, CZ), BF16)])
+        + [dma((8,))] + [dma((4,))] * 4 + [dma((2, GX - 1))] * 2 + [dma((2, GY - 1))] * 2,
         compiler_params=pltpu.CompilerParams(vmem_limit_bytes=LIMIT, collective_id=0, has_side_effects=True),
-        name="launch",
+        name="advance",
     )(count, *ins)
-
-
-def call_settle(got, start, q_now, q_prev, jac):
-    return pl.pallas_call(
-        settle,
-        out_shape=shapes([PLANES] + PARTS + FACES),
-        in_specs=[VM] * 5,
-        out_specs=[VM] * 5,
-        scratch_shapes=vmem(
-            FACES + [((21, CY, NDEV * CAP), BF16), ((CY, NDEV * CAP), F32), ((NDEV * CAP, CZ), BF16)]
-        )
-        + [pltpu.SemaphoreType.DMA((4,))] * 2,
-        compiler_params=pltpu.CompilerParams(vmem_limit_bytes=LIMIT, collective_id=1, has_side_effects=True),
-        name="settle",
-    )(got, start, q_now, q_prev, jac)
 
 
 def call_second(hi, lo, later, jac, halo_x, halo_y, km_hi, km_lo):
@@ -410,11 +429,10 @@
 
 
 def body(q_now, q_prev, jacobian, flux_split, donor_base, donor_frac, fringe_dest, receptor_cell, fringe_count):
-    got, start, km_hi, km_lo = call_launch(
+    later, hi, lo, halo_x, halo_y, km_hi, km_lo = call_advance(
         fringe_count, flux_split.transpose(0, 2, 1, 3), q_now, q_prev, jacobian, donor_base.reshape(1, ROWS),
         donor_frac, fringe_dest.reshape(1, ROWS), receptor_cell.reshape(1, ROWS),
     )
-    later, hi, lo, halo_x, halo_y = call_settle(got, start, q_now, q_prev, jacobian)
     return call_second(hi, lo, later, jacobian, halo_x, halo_y, km_hi, km_lo)
 
 

time: 42.9 us -> 35.2 us (0.82)
  the two profiles are of different devices: /device:TPU:0 before, /device:TPU:1 now
where the time goes in v2:
time: 35.2 us; the launch traced here: 35.1 us
  Pallas kernels  34.5 us (98%)
  between operations  0.68 us (2%)
    pallas_call x1, Pallas kernels, call_advance(): pl.pallas_call(advance, out_shape=shapes([PLANES] + PARTS + FACES + MATRI...  31.6 us
    pallas_call x1, Pallas kernels, call_second(): pl.pallas_call(second, out_shape=jax.ShapeDtypeStruct((V, CX, CY, CZ), F3...  2.9 us

profile of v2, /device:TPU:1, one launch (start us, length us, event | category | flops | bytes accessed | tf_op | source)
XLA Modules:
  0.0 35.1 jit_solution(10081931611482834487)
XLA Ops:
  0.7 0.0 copy-start
  0.7 31.6 %advance.1 = (f32[16,80,256]{2,1,0:T(8,128)S(1)}, bf16[16,80,256]{2,1,0:T(8,128)(2,1)S(1)}, bf16[16,80,256]{2,1,0:T(8,128)(2,1)S(1)}, f32[2,80,256]{2,1,0:T(8,12...) custom-call(s32[1]{0:T(128)S(6)} %copy.10.count, ...), custom_call_target="tpu_custom_call" | custom-call | tf_op jit(solution)/shard_map/advance/pallas_call | solution.py:405
  32.2 0.0 copy-done
  32.2 2.9 %second.1 = f32[5,16,16,256]{3,2,1,0:T(8,128)} custom-call(bf16[16,80,256]{2,1,0:T(8,128)(2,1)S(1)} %get-tuple-element.12.hi, bf16[16,80,256]{2,1,0:T(8,128)(2,1)S(1)} %get-tuple-element.13.lo, f32[16,80,256]{2,1,0:T(8,128)S(1)} %get-tuple-element.14.later, f32[16,16,256]{2,1,0:T(8,128)S(1)} %copy-done, f32[2,80,256]{2,1,0:T(8,128)S(1)} %get-tuple-element.15.halo_x, ...), custom_call_target="tpu_custom_call" | custom-call | tf_op jit(solution)/shard_map/second/pallas_call | solution.py:421
Async XLA Ops:
  0.7 31.6 %copy-start = (f32[16,16,256]{2,1,0:T(8,128)S(1)}, f32[16,16,256]{2,1,0:T(8,128)}, u32[]{:S(2)}) copy-start(f32[16,16,256]{2,1,0:T(8,128)} %jac.1) | copy-start | bytes 786436

commit v3 on v2

--- a/solution.py
+++ b/solution.py
@@ -68,20 +68,22 @@
     return jnp.concatenate(mains + ups + downs, axis=0)
 
 
-def y_faces(planes):
-    pad = [jnp.zeros((8 - V, CZ), F32)]
-    return [jnp.concatenate([p[y : y + 1, :] for p in planes] + pad, axis=0) for y in (0, CY - 1)]
-
-
 def beyond(halo_x, halo_y):
     ix, iy = lax.axis_index("gx"), lax.axis_index("gy")
     nx, ny = lax.axis_size("gx"), lax.axis_size("gy")
     keep_x = [jnp.where(ix > 0, 1.0, 0.0), jnp.where(ix < nx - 1, 1.0, 0.0)]
     keep_y = [jnp.where(iy > 0, 1.0, 0.0), jnp.where(iy < ny - 1, 1.0, 0.0)]
     ends = [two(halo_x[side] * keep_x[side]) for side in range(2)]
-    rows = [
-        two(jnp.concatenate([halo_y[side, x] * keep_y[side] for side in range(2)], axis=0)) for x in range(CX)
-    ]
+    pad = jnp.zeros((8 - V, CZ), F32)
+
+    def row(x):
+        tiles = []
+        for side in range(2):
+            both = [halo_y[side, h, pl.ds(x, V, stride=CX), :] for h in range(2)]
+            tiles += [jnp.concatenate(both, axis=1) * keep_y[side], pad]
+        return two(jnp.concatenate(tiles, axis=0))
+
+    rows = [row(x) for x in range(CX)]
     return ends, rows
 
 
@@ -107,17 +109,21 @@
         peer_y = lax.rem(iy + step + GY, GY)
         copies.append(
             pltpu.make_async_remote_copy(
-                face_x.at[side], halo_x.at[1 - side], send.at[side], recv.at[side],
+                face_x.at[side], halo_x.at[1 - side], send.at[0], recv.at[0],
                 device_id=(peer_x, iy), device_id_type=MESH,
             )
         )
         copies.append(
             pltpu.make_async_remote_copy(
-                face_y.at[side], halo_y.at[1 - side], send.at[2 + side], recv.at[2 + side],
+                face_y.at[side], halo_y.at[1 - side], send.at[1], recv.at[1],
                 device_id=(ix, peer_y), device_id_type=MESH,
             )
         )
     return copies
+
+
+def arrived(ref, sem):
+    pltpu.make_async_copy(ref, ref, sem).wait()
 
 
 def ranks(onehot, onehot_b):
@@ -188,8 +194,8 @@
     loads = [
         pltpu.make_async_copy(a, b, load.at[i])
         for i, (a, b) in enumerate(
-            [(dest_h, dest), (base_h, base), (frac_h, frac), (prev_h, q_prev), (now_h, q_now), (cell_h, cell),
-             (flux_h, flux), (jac_h, jac)]
+            [(dest_h, dest), (base_h, base), (frac_h, frac), (flux_h, flux), (cell_h, cell), (prev_h, q_prev),
+             (now_h, q_now), (jac_h, jac)]
         )
     ]
     for copy in loads:
@@ -206,14 +212,13 @@
             to = lax.rem(ix + k, GX)
             copies.append(
                 pltpu.make_async_remote_copy(
-                    sent.at[wave, to], mid.at[wave, ix], send_a.at[wave, k - 1], recv_a.at[wave, k - 1],
+                    sent.at[wave, to], mid.at[wave, ix], send_a.at[wave], recv_a.at[wave],
                     device_id=(to, iy), device_id_type=MESH,
                 )
             )
         for copy in copies:
             copy.start()
         mid[wave, ix] = sent[wave, ix]
-        return copies
 
     def along_gy(wave):
         copies = []
@@ -221,16 +226,15 @@
             to = lax.rem(iy + k, GY)
             copies.append(
                 pltpu.make_async_remote_copy(
-                    mid.at[wave, :, to], got.at[wave, iy], send_b.at[wave, k - 1], recv_b.at[wave, k - 1],
+                    mid.at[wave, :, to], got.at[wave, iy], send_b.at[wave], recv_b.at[wave],
                     device_id=(ix, to), device_id_type=MESH,
                 )
             )
         for copy in copies:
             copy.start()
         got[wave, iy] = mid[wave, :, iy]
-        return copies
-
-    for copy in loads[:3]:
+
+    for copy in loads[:5]:
         copy.wait()
     live = iota((1, ROWS), 1) < count[0]
     where_to = jnp.where(live, dest[...], NDEV)
@@ -238,7 +242,9 @@
     onehot_b = onehot.astype(BF16)
     slots = ranks(onehot, onehot_b)
     stencils(base, frac, z_parts, w_xy)
-    loads[3].wait()
+    hi, lo = two(flux_matrix(flux))
+    km_hi[...] = hi
+    km_lo[...] = lo
     loads[5].wait()
     for x in range(CX):
         for v in range(V):
@@ -254,18 +260,18 @@
     sent[0, :, :, 0, :] = by_block(packed, 2)
 
     pl.semaphore_wait(barrier, len(peers))
-    first_a = along_gx(0)
-    for i in (4, 6, 7):
-        loads[i].wait()
+    along_gx(0)
+    for copy in loads[6:]:
+        copy.wait()
     for x in range(CX):
         for v in range(V):
             hi, lo = two(q_now[v, x])
             now_hi[x, v * CY : (v + 1) * CY, :] = hi
             now_lo[x, v * CY : (v + 1) * CY, :] = lo
-        lo_y, hi_y = y_faces([q_now[v, x] for v in range(V)])
-        face_y[0, x] = lo_y
-        face_y[1, x] = hi_y
     for v in range(V):
+        for side, y in ((0, 0), (1, CY - 1)):
+            for h in range(2):
+                face_y[side, h, v * CX : (v + 1) * CX, :] = q_now[v, :, y, h * 128 : (h + 1) * 128]
         face_x[0, v * CY : (v + 1) * CY, :] = q_now[v, 0]
         face_x[1, v * CY : (v + 1) * CY, :] = q_now[v, CX - 1]
     faces = face_copies(ix, iy, face_x, face_y, halo_x, halo_y, send, recv)
@@ -274,18 +280,14 @@
     packed = jnp.zeros((10 * CAP, NDEV), F32)
     for c in range(0, 2):
         packed = packed + donate(c, now_hi, now_lo, z_parts, w_xy, slots, onehot_b, ())
-    for copy in first_a:
-        copy.wait_recv()
-    first_b = along_gy(0)
+    arrived(mid.at[0, pl.ds(0, GX - 1)], recv_a.at[0])
+    along_gy(0)
     for c in range(2, 4):
         packed = packed + donate(c, now_hi, now_lo, z_parts, w_xy, slots, onehot_b, ())
     sent[1, :, :, 0, :] = by_block(packed, 0)
-    second_a = along_gx(1)
-    hi, lo = two(flux_matrix(flux))
-    km_hi[...] = hi
-    km_lo[...] = lo
-    for copy in faces:
-        copy.wait()
+    along_gx(1)
+    arrived(halo_x, recv.at[0])
+    arrived(halo_y, recv.at[1])
     ends, rows = beyond(halo_x, halo_y)
     for x in range(CX):
         flux_x = flux_of(x, km_hi, km_lo, now_hi, now_lo, ends, rows)
@@ -293,11 +295,9 @@
         for v in range(V):
             part = slice(v * CY, (v + 1) * CY)
             start[x, part, :] = q_now[v, x] - scale * (flux_x[part] + (q_prev[v, x] - q_now[v, x]))
-    for copy in second_a:
-        copy.wait_recv()
-    second_b = along_gy(1)
-    for copy in first_b:
-        copy.wait_recv()
+    arrived(mid.at[1, pl.ds(0, GX - 1)], recv_a.at[1])
+    along_gy(1)
+    arrived(got.at[0, pl.ds(0, GY - 1)], recv_b.at[0])
 
     def spread(wave):
         rows = got[wave, :, :, 0, :].reshape(NDEV, 128)
@@ -335,7 +335,6 @@
             x = group * GROUP + j
             scale = 0.2 * jac[x]
             hits = rows_of(landed, j, 11, 10)
-            fresh = []
             for v in range(V):
                 part = slice(v * CY, (v + 1) * CY)
                 q, qp = q_now[v, x], q_prev[v, x]
@@ -345,17 +344,16 @@
                 hi_out[x, part, :] = hi
                 lo_out[x, part, :] = lo
                 later[x, part, :] = w - scale * ((3.0 * w - 4.0 * q + qp) + 2.0 * (hits * w))
-                fresh.append(w)
+                for side, y in ((0, 0), (1, CY - 1)):
+                    for h in range(2):
+                        row = w[y : y + 1, h * 128 : (h + 1) * 128]
+                        face2_y[side, h, v * CX + x : v * CX + x + 1, :] = row
                 if x in (0, CX - 1):
                     face2_x[0 if x == 0 else 1, part, :] = w
-            lo_y, hi_y = y_faces(fresh)
-            face2_y[0, x] = lo_y
-            face2_y[1, x] = hi_y
     faces2 = face_copies(ix, iy, face2_x, face2_y, halo2_x, halo2_y, send2, recv2)
     for copy in faces2:
         copy.start()
-    for copy in second_b:
-        copy.wait_recv()
+    arrived(got.at[1, pl.ds(0, GY - 1)], recv_b.at[1])
     spread(1)
     for group in range(CX // GROUP):
         landed = landing(group, 11, 21)
@@ -366,26 +364,34 @@
                 part = slice(v * CY, (v + 1) * CY)
                 target = rows_of(landed, j, 10, v) + rows_of(landed, j, 10, V + v)
                 later[x, part, :] = later[x, part, :] + scale * target
-    for copy in first_a + first_b + second_a + second_b:
-        copy.wait_send()
-    for copy in faces2:
-        copy.wait()
-
-
-def second(hi, lo, later, jac, halo_x, halo_y, km_hi, km_lo, out):
+    for wave in range(2):
+        arrived(sent.at[wave, pl.ds(0, GX - 1)], send_a.at[wave])
+        arrived(got.at[wave, pl.ds(0, GY - 1)], send_b.at[wave])
+    arrived(face_x, send.at[0])
+    arrived(face_y, send.at[1])
+    arrived(face2_x, send2.at[0])
+    arrived(face2_y, send2.at[1])
+    arrived(halo2_x, recv2.at[0])
+    arrived(halo2_y, recv2.at[1])
+
+
+def second(hi, lo, later, jac, halo_x, halo_y, km_hi, km_lo, out, plane, store):
     ends, rows = beyond(halo_x, halo_y)
     for x in range(CX):
         flux = flux_of(x, km_hi, km_lo, hi, lo, ends, rows)
         scale = 0.2 * jac[x]
         for v in range(V):
             part = slice(v * CY, (v + 1) * CY)
-            out[v, x] = later[x, part, :] - scale * flux[part]
+            plane[x, v] = later[x, part, :] - scale * flux[part]
+        pltpu.make_async_copy(plane.at[x], out.at[:, x], store.at[x]).start()
+    for x in range(CX):
+        pltpu.make_async_copy(plane.at[x], out.at[:, x], store.at[x]).wait()
 
 
 VM = pl.BlockSpec(memory_space=pltpu.VMEM)
 SM = pl.BlockSpec(memory_space=pltpu.SMEM)
 HB = pl.BlockSpec(memory_space=pltpu.HBM)
-FACES = [((2, VY, CZ), F32), ((2, CX, 8, CZ), F32)]
+FACES = [((2, VY, CZ), F32), ((2, 2, VY, 128), F32)]
 PLANES = ((CX, VY, CZ), F32)
 PARTS = [((CX, VY, CZ), BF16)] * 2
 MATRIX = [((3 * VY, 256), BF16)] * 2
@@ -411,7 +417,7 @@
         + vmem(PARTS * 2 + [PLANES, ((4, 3 * CZ, CHUNK), BF16), ((4, CX, CY, CHUNK), F32)])
         + vmem([((2, GX, GY, 1, 128), F32)] * 2 + [((2, GY, GX, 1, 128), F32)] + FACES * 3)
         + vmem([((21, CY, NDEV * CAP), BF16), ((CY, NDEV * CAP), F32), ((NDEV * CAP, CZ), BF16)])
-        + [dma((8,))] + [dma((4,))] * 4 + [dma((2, GX - 1))] * 2 + [dma((2, GY - 1))] * 2,
+        + [dma((8,))] + [dma((2,))] * 8,
         compiler_params=pltpu.CompilerParams(vmem_limit_bytes=LIMIT, collective_id=0, has_side_effects=True),
         name="advance",
     )(count, *ins)
@@ -422,7 +428,8 @@
         second,
         out_shape=jax.ShapeDtypeStruct((V, CX, CY, CZ), F32),
         in_specs=[VM] * 8,
-        out_specs=VM,
+        out_specs=HB,
+        scratch_shapes=[pltpu.VMEM((CX, V, CY, CZ), F32), pltpu.SemaphoreType.DMA((CX,))],
         compiler_params=pltpu.CompilerParams(vmem_limit_bytes=LIMIT),
         name="second",
     )(hi, lo, later, jac, halo_x, halo_y, km_hi, km_lo)

time: 35.2 us -> 33.2 us (0.943)
  Pallas kernels: 34.5 us -> 32.2 us
    pallas_call x1, Pallas kernels: 31.6 us -> 29.5 us  [call_advance(): pl.pallas_call(advance, out_shape=shapes([PLANES] + PARTS + FACES + MATRI...]
where the time goes in v3:
time: 33.2 us; the launch traced here: 33.1 us
  Pallas kernels  32.2 us (97%)
  between operations  0.84 us (3%)
    pallas_call x1, Pallas kernels, call_advance(): pl.pallas_call(advance, out_shape=shapes([PLANES] + PARTS + FACES + MATRI...  29.5 us
    pallas_call x1, Pallas kernels, call_second(): pl.pallas_call(second, out_shape=jax.ShapeDtypeStruct((V, CX, CY, CZ), F3...  2.69 us

profile of v3, /device:TPU:1, one launch (start us, length us, event | category | flops | bytes accessed | tf_op | source)
XLA Modules:
  0.0 33.1 jit_solution(13323445714670252333)
XLA Ops:
  0.7 0.0 copy-start
  0.7 29.5 %advance.1 = (f32[16,80,256]{2,1,0:T(8,128)S(1)}, bf16[16,80,256]{2,1,0:T(8,128)(2,1)S(1)}, bf16[16,80,256]{2,1,0:T(8,128)(2,1)S(1)}, f32[2,80,256]{2,1,0:T(8,12...) custom-call(s32[1]{0:T(128)S(6)} %copy.10.count, ...), custom_call_target="tpu_custom_call" | custom-call | tf_op jit(solution)/shard_map/advance/pallas_call | solution.py:411
  30.2 0.0 copy-done
  30.2 2.7 %second.1 = f32[5,16,16,256]{3,2,1,0:T(8,128)} custom-call(bf16[16,80,256]{2,1,0:T(8,128)(2,1)S(1)} %get-tuple-element.12.hi, bf16[16,80,256]{2,1,0:T(8,128)(2,1)S(1)} %get-tuple-element.13.lo, f32[16,80,256]{2,1,0:T(8,128)S(1)} %get-tuple-element.14.later, f32[16,16,256]{2,1,0:T(8,128)S(1)} %copy-done, f32[2,80,256]{2,1,0:T(8,128)S(1)} %get-tuple-element.15.halo_x, ...), custom_call_target="tpu_custom_call" | custom-call | tf_op jit(solution)/shard_map/second/pallas_call | solution.py:427
Async XLA Ops:
  0.7 29.6 %copy-start = (f32[16,16,256]{2,1,0:T(8,128)S(1)}, f32[16,16,256]{2,1,0:T(8,128)}, u32[]{:S(2)}) copy-start(f32[16,16,256]{2,1,0:T(8,128)} %jac.1) | copy-start | bytes 786436

commit v4 on v3

--- a/solution.py
+++ b/solution.py
@@ -16,6 +16,7 @@
 VY = V * CY
 CHUNK = 256
 GROUP = 4
+HALF = CX // 2
 LIMIT = 48 * 1024 * 1024
 
 
@@ -49,6 +50,7 @@
     mid = (block == 1).astype(F32)
     near = ((block == 1) | (block == 3)).astype(F32)
     w_mid, w_back, w_fwd = here * mid, back * near, fwd * near
+    w_any = here * (block < 3).astype(F32)
     w_left, w_right = here * (block == 0).astype(F32), here * (block == 2).astype(F32)
     mains, ups, downs = [], [], []
     for a in range(V):
@@ -63,9 +65,12 @@
         mains.append(
             centre * w_mid - row[1, 0] * w_back + row[1, 1] * w_fwd - row[0, 0] * w_left + row[0, 1] * w_right
         )
-        ups.append(row[2, 1] * w_mid)
-        downs.append(row[2, 0] * w_mid)
-    return jnp.concatenate(mains + ups + downs, axis=0)
+        ups.append(row[2, 1] * w_any)
+        downs.append(row[2, 0] * w_any)
+    hi, lo = two(jnp.concatenate(mains, axis=0))
+    along = jnp.concatenate(ups + downs, axis=0)
+    top = along.astype(BF16).astype(F32)
+    return jnp.concatenate([hi, lo], axis=0), jnp.where(block == 1, along - top, top).astype(BF16)
 
 
 def beyond(halo_x, halo_y):
@@ -79,7 +84,7 @@
     def row(x):
         tiles = []
         for side in range(2):
-            both = [halo_y[side, h, pl.ds(x, V, stride=CX), :] for h in range(2)]
+            both = [halo_y[x // HALF, side, h, pl.ds(x % HALF, V, stride=HALF), :] for h in range(2)]
             tiles += [jnp.concatenate(both, axis=1) * keep_y[side], pad]
         return two(jnp.concatenate(tiles, axis=0))
 
@@ -87,36 +92,41 @@
     return ends, rows
 
 
-def flux_of(x, km_hi, km_lo, hi, lo, ends, rows):
+def flux_of(x, km_xy, km_z, hi, lo, ends, rows):
     def tile(ref, part):
         left = ends[0][part] if x == 0 else ref[x - 1]
         right = ends[1][part] if x == CX - 1 else ref[x + 1]
         return jnp.concatenate([left, ref[x], right, rows[x][part]], axis=0)
 
-    top, low = tile(hi, 0), tile(lo, 1)
-    total = dot(km_hi[...], top) + dot(km_lo[...], top) + dot(km_hi[...], low)
+    both = dot(km_xy[...], tile(hi, 0))
+    total = both[:VY] + both[VY:] + dot(km_xy[:VY], tile(lo, 1))
+    along = dot(km_z[:, : 3 * VY], jnp.concatenate([hi[x], hi[x], lo[x]], axis=0))
     z = iota((VY, CZ), 1)
-    fwd = jnp.where(z == CZ - 1, 0.0, pltpu.roll(total[VY : 2 * VY], CZ - 1, 1))
-    back = jnp.where(z == 0, 0.0, pltpu.roll(total[2 * VY :], 1, 1))
-    return total[:VY] + fwd - back
-
-
-def face_copies(ix, iy, face_x, face_y, halo_x, halo_y, send, recv):
+    fwd = jnp.where(z == CZ - 1, 0.0, pltpu.roll(along[:VY], CZ - 1, 1))
+    back = jnp.where(z == 0, 0.0, pltpu.roll(along[VY:], 1, 1))
+    return total + fwd - back
+
+
+def x_copies(ix, iy, face_x, halo_x, send, recv):
     copies = []
     for side in range(2):
-        step = 2 * side - 1
-        peer_x = lax.rem(ix + step + GX, GX)
-        peer_y = lax.rem(iy + step + GY, GY)
+        peer = lax.rem(ix + 2 * side - 1 + GX, GX)
         copies.append(
             pltpu.make_async_remote_copy(
-                face_x.at[side], halo_x.at[1 - side], send.at[0], recv.at[0],
-                device_id=(peer_x, iy), device_id_type=MESH,
+                face_x.at[side], halo_x.at[1 - side], send, recv, device_id=(peer, iy), device_id_type=MESH
             )
         )
+    return copies
+
+
+def y_copies(ix, iy, face_y, halo_y, piece, send, recv):
+    copies = []
+    for side in range(2):
+        peer = lax.rem(iy + 2 * side - 1 + GY, GY)
         copies.append(
             pltpu.make_async_remote_copy(
-                face_y.at[side], halo_y.at[1 - side], send.at[1], recv.at[1],
-                device_id=(ix, peer_y), device_id_type=MESH,
+                face_y.at[piece, side], halo_y.at[piece, 1 - side], send, recv,
+                device_id=(ix, peer), device_id_type=MESH,
             )
         )
     return copies
@@ -187,19 +197,21 @@
 
 
 def advance(count, flux_h, now_h, prev_h, jac_h, base_h, frac_h, dest_h, cell_h,
-            later, hi_out, lo_out, halo2_x, halo2_y, km_hi, km_lo,
+            later, hi_out, lo_out, halo2_x, halo2_y, km_xy, km_z,
             flux, q_now, q_prev, jac, base, frac, dest, cell, now_hi, now_lo, prev_hi, prev_lo, start, z_parts, w_xy,
             sent, mid, got, face_x, face_y, halo_x, halo_y, face2_x, face2_y, parts, places, at_z,
             load, send, recv, send2, recv2, send_a, recv_a, send_b, recv_b):
     loads = [
         pltpu.make_async_copy(a, b, load.at[i])
         for i, (a, b) in enumerate(
-            [(dest_h, dest), (base_h, base), (frac_h, frac), (flux_h, flux), (cell_h, cell), (prev_h, q_prev),
-             (now_h, q_now), (jac_h, jac)]
+            [(dest_h, dest), (base_h, base), (frac_h, frac), (flux_h, flux), (cell_h, cell), (now_h, q_now),
+             (jac_h, jac)]
         )
     ]
-    for copy in loads:
+    for copy in loads[:5]:
         copy.start()
+    for v in range(V):
+        pltpu.make_async_copy(prev_h.at[v], q_prev.at[v], load.at[7]).start()
     ix, iy = lax.axis_index("gx"), lax.axis_index("gy")
     peers = [(lax.rem(ix + k, GX), iy) for k in range(1, GX)] + [(ix, lax.rem(iy + k, GY)) for k in range(1, GY)]
     barrier = pltpu.get_barrier_semaphore()
@@ -242,10 +254,12 @@
     onehot_b = onehot.astype(BF16)
     slots = ranks(onehot, onehot_b)
     stencils(base, frac, z_parts, w_xy)
-    hi, lo = two(flux_matrix(flux))
-    km_hi[...] = hi
-    km_lo[...] = lo
-    loads[5].wait()
+    mat_xy, mat_z = flux_matrix(flux)
+    km_xy[...] = mat_xy
+    km_z[...] = mat_z
+    arrived(q_prev, load.at[7])
+    for copy in loads[5:]:
+        copy.start()
     for x in range(CX):
         for v in range(V):
             hi, lo = two(q_prev[v, x])
@@ -261,7 +275,7 @@
 
     pl.semaphore_wait(barrier, len(peers))
     along_gx(0)
-    for copy in loads[6:]:
+    for copy in loads[5:]:
         copy.wait()
     for x in range(CX):
         for v in range(V):
@@ -271,12 +285,17 @@
     for v in range(V):
         for side, y in ((0, 0), (1, CY - 1)):
             for h in range(2):
-                face_y[side, h, v * CX : (v + 1) * CX, :] = q_now[v, :, y, h * 128 : (h + 1) * 128]
+                for p in range(2):
+                    face_y[p, side, h, v * HALF : (v + 1) * HALF, :] = q_now[
+                        v, p * HALF : (p + 1) * HALF, y, h * 128 : (h + 1) * 128
+                    ]
         face_x[0, v * CY : (v + 1) * CY, :] = q_now[v, 0]
         face_x[1, v * CY : (v + 1) * CY, :] = q_now[v, CX - 1]
-    faces = face_copies(ix, iy, face_x, face_y, halo_x, halo_y, send, recv)
-    for copy in faces:
+    for copy in x_copies(ix, iy, face_x, halo_x, send.at[0], recv.at[0]):
         copy.start()
+    for p in range(2):
+        for copy in y_copies(ix, iy, face_y, halo_y, p, send.at[1], recv.at[1]):
+            copy.start()
     packed = jnp.zeros((10 * CAP, NDEV), F32)
     for c in range(0, 2):
         packed = packed + donate(c, now_hi, now_lo, z_parts, w_xy, slots, onehot_b, ())
@@ -290,13 +309,11 @@
     arrived(halo_y, recv.at[1])
     ends, rows = beyond(halo_x, halo_y)
     for x in range(CX):
-        flux_x = flux_of(x, km_hi, km_lo, now_hi, now_lo, ends, rows)
+        flux_x = flux_of(x, km_xy, km_z, now_hi, now_lo, ends, rows)
         scale = 0.2 * jac[x]
         for v in range(V):
             part = slice(v * CY, (v + 1) * CY)
             start[x, part, :] = q_now[v, x] - scale * (flux_x[part] + (q_prev[v, x] - q_now[v, x]))
-    arrived(mid.at[1, pl.ds(0, GX - 1)], recv_a.at[1])
-    along_gy(1)
     arrived(got.at[0, pl.ds(0, GY - 1)], recv_b.at[0])
 
     def spread(wave):
@@ -347,11 +364,18 @@
                 for side, y in ((0, 0), (1, CY - 1)):
                     for h in range(2):
                         row = w[y : y + 1, h * 128 : (h + 1) * 128]
-                        face2_y[side, h, v * CX + x : v * CX + x + 1, :] = row
+                        at = v * HALF + x % HALF
+                        face2_y[x // HALF, side, h, at : at + 1, :] = row
                 if x in (0, CX - 1):
                     face2_x[0 if x == 0 else 1, part, :] = w
-    faces2 = face_copies(ix, iy, face2_x, face2_y, halo2_x, halo2_y, send2, recv2)
-    for copy in faces2:
+        if group == 0:
+            arrived(mid.at[1, pl.ds(0, GX - 1)], recv_a.at[1])
+            along_gy(1)
+        if group % 2 == 1:
+            p = group // 2
+            for copy in y_copies(ix, iy, face2_y, halo2_y, p, send2.at[1 + p], recv2.at[1 + p]):
+                copy.start()
+    for copy in x_copies(ix, iy, face2_x, halo2_x, send2.at[0], recv2.at[0]):
         copy.start()
     arrived(got.at[1, pl.ds(0, GY - 1)], recv_b.at[1])
     spread(1)
@@ -370,15 +394,16 @@
     arrived(face_x, send.at[0])
     arrived(face_y, send.at[1])
     arrived(face2_x, send2.at[0])
-    arrived(face2_y, send2.at[1])
+    for p in range(2):
+        arrived(face2_y.at[p], send2.at[1 + p])
+        arrived(halo2_y.at[p], recv2.at[1 + p])
     arrived(halo2_x, recv2.at[0])
-    arrived(halo2_y, recv2.at[1])
-
-
-def second(hi, lo, later, jac, halo_x, halo_y, km_hi, km_lo, out, plane, store):
+
+
+def second(hi, lo, later, jac, halo_x, halo_y, km_xy, km_z, out, plane, store):
     ends, rows = beyond(halo_x, halo_y)
     for x in range(CX):
-        flux = flux_of(x, km_hi, km_lo, hi, lo, ends, rows)
+        flux = flux_of(x, km_xy, km_z, hi, lo, ends, rows)
         scale = 0.2 * jac[x]
         for v in range(V):
             part = slice(v * CY, (v + 1) * CY)
@@ -391,10 +416,10 @@
 VM = pl.BlockSpec(memory_space=pltpu.VMEM)
 SM = pl.BlockSpec(memory_space=pltpu.SMEM)
 HB = pl.BlockSpec(memory_space=pltpu.HBM)
-FACES = [((2, VY, CZ), F32), ((2, 2, VY, 128), F32)]
+FACES = [((2, VY, CZ), F32), ((2, 2, 2, V * HALF, 128), F32)]
 PLANES = ((CX, VY, CZ), F32)
 PARTS = [((CX, VY, CZ), BF16)] * 2
-MATRIX = [((3 * VY, 256), BF16)] * 2
+MATRIX = [((2 * VY, 256), BF16)] * 2
 
 
 def shapes(entries):
@@ -417,13 +442,13 @@
         + vmem(PARTS * 2 + [PLANES, ((4, 3 * CZ, CHUNK), BF16), ((4, CX, CY, CHUNK), F32)])
         + vmem([((2, GX, GY, 1, 128), F32)] * 2 + [((2, GY, GX, 1, 128), F32)] + FACES * 3)
         + vmem([((21, CY, NDEV * CAP), BF16), ((CY, NDEV * CAP), F32), ((NDEV * CAP, CZ), BF16)])
-        + [dma((8,))] + [dma((2,))] * 8,
+        + [dma((8,))] + [dma((2,))] * 2 + [dma((3,))] * 2 + [dma((2,))] * 4,
         compiler_params=pltpu.CompilerParams(vmem_limit_bytes=LIMIT, collective_id=0, has_side_effects=True),
         name="advance",
     )(count, *ins)
 
 
-def call_second(hi, lo, later, jac, halo_x, halo_y, km_hi, km_lo):
+def call_second(hi, lo, later, jac, halo_x, halo_y, km_xy, km_z):
     return pl.pallas_call(
         second,
         out_shape=jax.ShapeDtypeStruct((V, CX, CY, CZ), F32),
@@ -432,15 +457,15 @@
         scratch_shapes=[pltpu.VMEM((CX, V, CY, CZ), F32), pltpu.SemaphoreType.DMA((CX,))],
         compiler_params=pltpu.CompilerParams(vmem_limit_bytes=LIMIT),
         name="second",
-    )(hi, lo, later, jac, halo_x, halo_y, km_hi, km_lo)
+    )(hi, lo, later, jac, halo_x, halo_y, km_xy, km_z)
 
 
 def body(q_now, q_prev, jacobian, flux_split, donor_base, donor_frac, fringe_dest, receptor_cell, fringe_count):
-    later, hi, lo, halo_x, halo_y, km_hi, km_lo = call_advance(
+    later, hi, lo, halo_x, halo_y, km_xy, km_z = call_advance(
         fringe_count, flux_split.transpose(0, 2, 1, 3), q_now, q_prev, jacobian, donor_base.reshape(1, ROWS),
         donor_frac, fringe_dest.reshape(1, ROWS), receptor_cell.reshape(1, ROWS),
     )
-    return call_second(hi, lo, later, jacobian, halo_x, halo_y, km_hi, km_lo)
+    return call_second(hi, lo, later, jacobian, halo_x, halo_y, km_xy, km_z)
 
 
 def solution(mesh):

time: 33.2 us -> 33.6 us (1.012)
  Pallas kernels: 32.2 us -> 32.6 us
    pallas_call x1, Pallas kernels: 29.5 us -> 30.6 us  [call_advance(): pl.pallas_call(advance, out_shape=shapes([PLANES] + PARTS + FACES + MATRI...]
    pallas_call x1, Pallas kernels: 2.69 us -> 1.99 us  [call_second(): pl.pallas_call(second, out_shape=jax.ShapeDtypeStruct((V, CX, CY, CZ), F3...]
where the time goes in v4:
time: 33.6 us; the launch traced here: 33.4 us
  Pallas kernels  32.6 us (97%)
  between operations  0.84 us (2%)
    pallas_call x1, Pallas kernels, call_advance(): pl.pallas_call(advance, out_shape=shapes([PLANES] + PARTS + FACES + MATRI...  30.6 us
    pallas_call x1, Pallas kernels, call_second(): pl.pallas_call(second, out_shape=jax.ShapeDtypeStruct((V, CX, CY, CZ), F3...  1.99 us

profile of v4, /device:TPU:1, one launch (start us, length us, event | category | flops | bytes accessed | tf_op | source)
XLA Modules:
  0.0 33.4 jit_solution(3774228600352892296)
XLA Ops:
  0.7 0.0 copy-start
  0.7 30.6 %advance.1 = (f32[16,80,256]{2,1,0:T(8,128)S(1)}, bf16[16,80,256]{2,1,0:T(8,128)(2,1)S(1)}, bf16[16,80,256]{2,1,0:T(8,128)(2,1)S(1)}, f32[2,80,256]{2,1,0:T(8,12...) custom-call(s32[1]{0:T(128)S(6)} %copy.10.count, ...), custom_call_target="tpu_custom_call" | custom-call | tf_op jit(solution)/shard_map/advance/pallas_call | solution.py:436
  31.3 0.0 copy-done
  31.3 2.0 %second.1 = f32[5,16,16,256]{3,2,1,0:T(8,128)} custom-call(bf16[16,80,256]{2,1,0:T(8,128)(2,1)S(1)} %get-tuple-element.12.hi, bf16[16,80,256]{2,1,0:T(8,128)(2,1)S(1)} %get-tuple-element.13.lo, f32[16,80,256]{2,1,0:T(8,128)S(1)} %get-tuple-element.14.later, f32[16,16,256]{2,1,0:T(8,128)S(1)} %copy-done, f32[2,80,256]{2,1,0:T(8,128)S(1)} %get-tuple-element.15.halo_x, ...), custom_call_target="tpu_custom_call" | custom-call | tf_op jit(solution)/shard_map/second/pallas_call | solution.py:452
Async XLA Ops:
  0.7 30.6 %copy-start = (f32[16,16,256]{2,1,0:T(8,128)S(1)}, f32[16,16,256]{2,1,0:T(8,128)}, u32[]{:S(2)}) copy-start(f32[16,16,256]{2,1,0:T(8,128)} %jac.1) | copy-start | bytes 786436

commit v5 on v4

--- a/solution.py
+++ b/solution.py
@@ -297,14 +297,12 @@
         for copy in y_copies(ix, iy, face_y, halo_y, p, send.at[1], recv.at[1]):
             copy.start()
     packed = jnp.zeros((10 * CAP, NDEV), F32)
-    for c in range(0, 2):
-        packed = packed + donate(c, now_hi, now_lo, z_parts, w_xy, slots, onehot_b, ())
-    arrived(mid.at[0, pl.ds(0, GX - 1)], recv_a.at[0])
-    along_gy(0)
-    for c in range(2, 4):
+    for c in range(ROWS // CHUNK):
         packed = packed + donate(c, now_hi, now_lo, z_parts, w_xy, slots, onehot_b, ())
     sent[1, :, :, 0, :] = by_block(packed, 0)
     along_gx(1)
+    arrived(mid.at[0, pl.ds(0, GX - 1)], recv_a.at[0])
+    along_gy(0)
     arrived(halo_x, recv.at[0])
     arrived(halo_y, recv.at[1])
     ends, rows = beyond(halo_x, halo_y)
@@ -314,6 +312,8 @@
         for v in range(V):
             part = slice(v * CY, (v + 1) * CY)
             start[x, part, :] = q_now[v, x] - scale * (flux_x[part] + (q_prev[v, x] - q_now[v, x]))
+    arrived(mid.at[1, pl.ds(0, GX - 1)], recv_a.at[1])
+    along_gy(1)
     arrived(got.at[0, pl.ds(0, GY - 1)], recv_b.at[0])
 
     def spread(wave):
@@ -368,9 +368,6 @@
                         face2_y[x // HALF, side, h, at : at + 1, :] = row
                 if x in (0, CX - 1):
                     face2_x[0 if x == 0 else 1, part, :] = w
-        if group == 0:
-            arrived(mid.at[1, pl.ds(0, GX - 1)], recv_a.at[1])
-            along_gy(1)
         if group % 2 == 1:
             p = group // 2
             for copy in y_copies(ix, iy, face2_y, halo2_y, p, send2.at[1 + p], recv2.at[1 + p]):

time: 33.6 us -> 31.3 us (0.932)
  Pallas kernels: 32.6 us -> 30.3 us
    pallas_call x1, Pallas kernels: 30.6 us -> 28.3 us  [call_advance(): pl.pallas_call(advance, out_shape=shapes([PLANES] + PARTS + FACES + MATRI...]
where the time goes in v5:
time: 31.3 us; the launch traced here: 31.1 us
  Pallas kernels  30.3 us (97%)
  between operations  0.84 us (3%)
    pallas_call x1, Pallas kernels, call_advance(): pl.pallas_call(advance, out_shape=shapes([PLANES] + PARTS + FACES + MATRI...  28.3 us
    pallas_call x1, Pallas kernels, call_second(): pl.pallas_call(second, out_shape=jax.ShapeDtypeStruct((V, CX, CY, CZ), F3...  1.99 us

profile of v5, /device:TPU:1, one launch (start us, length us, event | category | flops | bytes accessed | tf_op | source)
XLA Modules:
  0.0 31.1 jit_solution(17516752315421473378)
XLA Ops:
  0.7 0.0 copy-start
  0.7 28.3 %advance.1 = (f32[16,80,256]{2,1,0:T(8,128)S(1)}, bf16[16,80,256]{2,1,0:T(8,128)(2,1)S(1)}, bf16[16,80,256]{2,1,0:T(8,128)(2,1)S(1)}, f32[2,80,256]{2,1,0:T(8,12...) custom-call(s32[1]{0:T(128)S(6)} %copy.10.count, ...), custom_call_target="tpu_custom_call" | custom-call | tf_op jit(solution)/shard_map/advance/pallas_call | solution.py:433
  29.0 0.0 copy-done
  29.0 2.0 %second.1 = f32[5,16,16,256]{3,2,1,0:T(8,128)} custom-call(bf16[16,80,256]{2,1,0:T(8,128)(2,1)S(1)} %get-tuple-element.12.hi, bf16[16,80,256]{2,1,0:T(8,128)(2,1)S(1)} %get-tuple-element.13.lo, f32[16,80,256]{2,1,0:T(8,128)S(1)} %get-tuple-element.14.later, f32[16,16,256]{2,1,0:T(8,128)S(1)} %copy-done, f32[2,80,256]{2,1,0:T(8,128)S(1)} %get-tuple-element.15.halo_x, ...), custom_call_target="tpu_custom_call" | custom-call | tf_op jit(solution)/shard_map/second/pallas_call | solution.py:449
Async XLA Ops:
  0.7 28.3 %copy-start = (f32[16,16,256]{2,1,0:T(8,128)S(1)}, f32[16,16,256]{2,1,0:T(8,128)}, u32[]{:S(2)}) copy-start(f32[16,16,256]{2,1,0:T(8,128)} %jac.1) | copy-start | bytes 786436

commit v6 on v5

--- a/solution.py
+++ b/solution.py
@@ -15,7 +15,7 @@
 GX, GY = 8, 16
 VY = V * CY
 CHUNK = 256
-GROUP = 4
+GROUP = 8
 HALF = CX // 2
 LIMIT = 48 * 1024 * 1024
 
@@ -368,10 +368,9 @@
                         face2_y[x // HALF, side, h, at : at + 1, :] = row
                 if x in (0, CX - 1):
                     face2_x[0 if x == 0 else 1, part, :] = w
-        if group % 2 == 1:
-            p = group // 2
-            for copy in y_copies(ix, iy, face2_y, halo2_y, p, send2.at[1 + p], recv2.at[1 + p]):
-                copy.start()
+    for p in range(2):
+        for copy in y_copies(ix, iy, face2_y, halo2_y, p, send2.at[1 + p], recv2.at[1 + p]):
+            copy.start()
     for copy in x_copies(ix, iy, face2_x, halo2_x, send2.at[0], recv2.at[0]):
         copy.start()
     arrived(got.at[1, pl.ds(0, GY - 1)], recv_b.at[1])

time: 31.3 us -> 30.7 us (0.981)
  Pallas kernels: 30.3 us -> 29.8 us
    pallas_call x1, Pallas kernels: 28.3 us -> 27.8 us  [call_advance(): pl.pallas_call(advance, out_shape=shapes([PLANES] + PARTS + FACES + MATRI...]
where the time goes in v6:
time: 30.7 us; the launch traced here: 30.6 us
  Pallas kernels  29.8 us (97%)
  between operations  0.84 us (3%)
    pallas_call x1, Pallas kernels, call_advance(): pl.pallas_call(advance, out_shape=shapes([PLANES] + PARTS + FACES + MATRI...  27.8 us
    pallas_call x1, Pallas kernels, call_second(): pl.pallas_call(second, out_shape=jax.ShapeDtypeStruct((V, CX, CY, CZ), F3...  1.99 us

profile of v6, /device:TPU:1, one launch (start us, length us, event | category | flops | bytes accessed | tf_op | source)
XLA Modules:
  0.0 30.6 jit_solution(6789575420329905604)
XLA Ops:
  0.7 0.0 copy-start
  0.7 27.8 %advance.1 = (f32[16,80,256]{2,1,0:T(8,128)S(1)}, bf16[16,80,256]{2,1,0:T(8,128)(2,1)S(1)}, bf16[16,80,256]{2,1,0:T(8,128)(2,1)S(1)}, f32[2,80,256]{2,1,0:T(8,12...) custom-call(s32[1]{0:T(128)S(6)} %copy.10.count, ...), custom_call_target="tpu_custom_call" | custom-call | tf_op jit(solution)/shard_map/advance/pallas_call | solution.py:432
  28.4 0.0 copy-done
  28.5 2.0 %second.1 = f32[5,16,16,256]{3,2,1,0:T(8,128)} custom-call(bf16[16,80,256]{2,1,0:T(8,128)(2,1)S(1)} %get-tuple-element.12.hi, bf16[16,80,256]{2,1,0:T(8,128)(2,1)S(1)} %get-tuple-element.13.lo, f32[16,80,256]{2,1,0:T(8,128)S(1)} %get-tuple-element.14.later, f32[16,16,256]{2,1,0:T(8,128)S(1)} %copy-done, f32[2,80,256]{2,1,0:T(8,128)S(1)} %get-tuple-element.15.halo_x, ...), custom_call_target="tpu_custom_call" | custom-call | tf_op jit(solution)/shard_map/second/pallas_call | solution.py:448
Async XLA Ops:
  0.7 27.8 %copy-start = (f32[16,16,256]{2,1,0:T(8,128)S(1)}, f32[16,16,256]{2,1,0:T(8,128)}, u32[]{:S(2)}) copy-start(f32[16,16,256]{2,1,0:T(8,128)} %jac.1) | copy-start | bytes 786436

commit v7 on v6

--- a/solution.py
+++ b/solution.py
@@ -234,7 +234,7 @@
 
     def along_gy(wave):
         copies = []
-        for k in range(1, GY):
+        for k in sorted(range(1, GY), key=lambda k: abs(k - GY // 2)):
             to = lax.rem(iy + k, GY)
             copies.append(
                 pltpu.make_async_remote_copy(
@@ -257,6 +257,7 @@
     mat_xy, mat_z = flux_matrix(flux)
     km_xy[...] = mat_xy
     km_z[...] = mat_z
+    parts[10] = jnp.ones((CY, NDEV * CAP), BF16)
     arrived(q_prev, load.at[7])
     for copy in loads[5:]:
         copy.start()
@@ -328,7 +329,6 @@
         return rows, turned
 
     rows, turned = spread(0)
-    parts[10] = jnp.ones((CY, NDEV * CAP), BF16)
     for s in range(CAP):
         lanes = slice(s * NDEV, (s + 1) * NDEV)
         places[:, lanes] = jnp.broadcast_to(turned[5 * CAP + s :][:1], (CY, NDEV))

time: 30.7 us -> 30.7 us (level)
  no operation moved by 1% of the time
where the time goes in v7:
time: 30.7 us; the launch traced here: 30.6 us
  Pallas kernels  29.7 us (97%)
  between operations  0.84 us (3%)
    pallas_call x1, Pallas kernels, call_advance(): pl.pallas_call(advance, out_shape=shapes([PLANES] + PARTS + FACES + MATRI...  27.7 us
    pallas_call x1, Pallas kernels, call_second(): pl.pallas_call(second, out_shape=jax.ShapeDtypeStruct((V, CX, CY, CZ), F3...  1.99 us

profile of v7, /device:TPU:1, one launch (start us, length us, event | category | flops | bytes accessed | tf_op | source)
XLA Modules:
  0.0 30.6 jit_solution(12210946232327053050)
XLA Ops:
  0.7 0.0 copy-start
  0.7 27.7 %advance.1 = (f32[16,80,256]{2,1,0:T(8,128)S(1)}, bf16[16,80,256]{2,1,0:T(8,128)(2,1)S(1)}, bf16[16,80,256]{2,1,0:T(8,128)(2,1)S(1)}, f32[2,80,256]{2,1,0:T(8,12...) custom-call(s32[1]{0:T(128)S(6)} %copy.10.count, ...), custom_call_target="tpu_custom_call" | custom-call | tf_op jit(solution)/shard_map/advance/pallas_call | solution.py:432
  28.4 0.0 copy-done
  28.4 2.0 %second.1 = f32[5,16,16,256]{3,2,1,0:T(8,128)} custom-call(bf16[16,80,256]{2,1,0:T(8,128)(2,1)S(1)} %get-tuple-element.12.hi, bf16[16,80,256]{2,1,0:T(8,128)(2,1)S(1)} %get-tuple-element.13.lo, f32[16,80,256]{2,1,0:T(8,128)S(1)} %get-tuple-element.14.later, f32[16,16,256]{2,1,0:T(8,128)S(1)} %copy-done, f32[2,80,256]{2,1,0:T(8,128)S(1)} %get-tuple-element.15.halo_x, ...), custom_call_target="tpu_custom_call" | custom-call | tf_op jit(solution)/shard_map/second/pallas_call | solution.py:448
Async XLA Ops:
  0.7 27.8 %copy-start = (f32[16,16,256]{2,1,0:T(8,128)S(1)}, f32[16,16,256]{2,1,0:T(8,128)}, u32[]{:S(2)}) copy-start(f32[16,16,256]{2,1,0:T(8,128)} %jac.1) | copy-start | bytes 786436
